TPU v7x, 512 devices: a whole 4x8x8 slice. The times are simulated.
512 devices in a mesh: ctx: 64 (over z, y_hi, core), head: 8 (over y_lo, x).
Axes of the slice: x: 4, y: 8 (y_hi: 4, y_lo: 2; y = y_hi * 2 + y_lo), z: 8, core: 2. Of those that a mesh axis runs over, the one named last changes fastest.
Arguments:
- query: bfloat16 [8192, 4096], P('ctx', 'head'), may hold values from -11 to 11
- key_proj: bfloat16 [8192, 1024], P(('ctx', 'head')), may hold values from -6 to 6
- value_proj: bfloat16 [8192, 1024], P(('ctx', 'head')), may hold values from -6 to 6
- d_out: bfloat16 [8192, 4096], P('ctx', 'head'), may hold values from -6 to 6
- block_doc: int32 [64], replicated, may hold values from 0 to 2, as said below
- block_mask: int32 [64, 64], replicated, may hold values 0 or 1
Outputs:
- attn_out: bfloat16 [8192, 4096], P('ctx', 'head')
- d_query: bfloat16 [8192, 4096], P('ctx', 'head')
- d_key: bfloat16 [8192, 1024], P(('ctx', 'head'))
- d_value: bfloat16 [8192, 1024], P(('ctx', 'head'))
Inputs may be any that keep to these rules, and one draw needn't show every extreme that they name: `block_doc`: ids never fall; each document spans 1 to 35 blocks and one spans exactly 35.
All inputs are finite; a program needn't handle non-finite values.
Results may differ from a plain program's by a relative error of at most 0.04.
Values may be sent and summed in bfloat16 or wider, within the bound.
No kernel may reach another device: no remote copies, remote signals or barrier semaphores. Data moves between devices by JAX's collectives and lax.ppermute only.
A program may use at most 64 MiB of HBM per device.

v0:
```python
import jax
import jax.numpy as jnp
import numpy as np
from jax import lax
from jax.sharding import PartitionSpec as P

HEAD_DIM = 128
Q_PER_KV = 4
BLOCK = 128


neg_fill = -1e30


def passed_along(block, axis, distance):
    devices = range(lax.axis_size(axis))
    route = [(i - distance, i) for i in devices if i - distance in devices]
    return lax.ppermute(block, axis, route)


def allowed_pairs(q_tok, k_tok, block_doc, block_mask):
    q_blk = q_tok // BLOCK
    k_blk = k_tok // BLOCK
    table = jnp.take(jnp.take(block_mask, q_blk, axis=0), k_blk, axis=1)
    same_doc = jnp.take(block_doc, q_blk)[:, None] == jnp.take(block_doc, k_blk)[None, :]
    earlier = (k_blk[None, :] < q_blk[:, None]) & (table == 1) & same_doc
    diagonal = (k_blk[None, :] == q_blk[:, None]) & (k_tok[None, :] <= q_tok[:, None])
    return earlier | diagonal


def sweep_keys(state, key_rows, value_rows, start, step_fn):
    count = key_rows.shape[0]
    width = 512
    turns = count // width

    def one_turn(turn, current):
        key_part = lax.dynamic_slice_in_dim(key_rows, turn * width, width, 0)
        value_part = lax.dynamic_slice_in_dim(value_rows, turn * width, width, 0)
        return step_fn(current, key_part, value_part, start + turn * width)

    return lax.fori_loop(0, turns, one_turn, state)


def body(query, key_proj, value_proj, d_out, block_doc, block_mask):
    q_count = query.shape[0]
    groups = query.shape[1] // (Q_PER_KV * HEAD_DIM)
    scale_qk = HEAD_DIM ** (-0.5)
    keys, values = (
        lax.all_to_all(key_proj, "head", split_axis=1, concat_axis=0, tiled=True),
        lax.all_to_all(value_proj, "head", split_axis=1, concat_axis=0, tiled=True),
    )
    q_tok = lax.axis_index("ctx") * q_count + jnp.arange(q_count, dtype=jnp.int32)
    n_keys = q_count * lax.axis_size("ctx")

    def heads_first(matrix):
        shaped = matrix.reshape(q_count, groups, Q_PER_KV, HEAD_DIM).transpose(1, 2, 0, 3)
        return shaped.reshape(groups, Q_PER_KV * q_count, HEAD_DIM)

    def rows_first(heads):
        shaped = heads.reshape(groups, Q_PER_KV, q_count, HEAD_DIM).transpose(2, 0, 1, 3)
        return shaped.reshape(q_count, groups * Q_PER_KV * HEAD_DIM)

    q_heads = heads_first(query)
    do_heads = heads_first(d_out)

    def mask_for(start, count):
        k_tok = start + jnp.arange(count, dtype=jnp.int32)
        return jnp.tile(allowed_pairs(q_tok, k_tok, block_doc, block_mask), (Q_PER_KV, 1))

    def forward_step(state, key_part, value_part, start):
        count = key_part.shape[0]
        allow = mask_for(start, count)

        def forward_compute(current):
            run_max, run_sum, accum = current
            key_three = key_part.reshape(count, groups, HEAD_DIM)
            value_three = value_part.reshape(count, groups, HEAD_DIM)
            scores = (
                jnp.einsum("gqd,kgd->gqk", q_heads, key_three, preferred_element_type=jnp.float32)
                * scale_qk
            )
            scores = jnp.where(allow[None], scores, neg_fill)
            new_max = jnp.maximum(run_max, jnp.max(scores, axis=-1, keepdims=True))
            factor = jnp.exp(run_max - new_max)
            expo = jnp.where(allow[None], jnp.exp(scores - new_max), 0.0)
            new_sum = run_sum * factor + jnp.sum(expo, axis=-1, keepdims=True)
            added = jnp.einsum(
                "gqk,kgd->gqd",
                expo.astype(jnp.bfloat16),
                value_three,
                preferred_element_type=jnp.float32,
            )
            return (new_max, new_sum, accum * factor + added)

        return lax.cond(jnp.any(allow), forward_compute, lambda current: current, state)

    init_fwd = (
        jnp.full((groups, Q_PER_KV * q_count, 1), neg_fill, jnp.float32),
        jnp.zeros((groups, Q_PER_KV * q_count, 1), jnp.float32),
        jnp.zeros((groups, Q_PER_KV * q_count, HEAD_DIM), jnp.float32),
    )
    all_keys, all_values = (
        lax.all_gather(keys, "ctx", axis=0, tiled=True),
        lax.all_gather(values, "ctx", axis=0, tiled=True),
    )
    fwd_state = sweep_keys(init_fwd, all_keys, all_values, 0, forward_step)
    run_max, run_sum, accum = fwd_state
    out_heads = (accum / run_sum).astype(jnp.bfloat16)
    log_total = run_max + jnp.log(run_sum)
    delta = jnp.sum(
        do_heads.astype(jnp.float32) * out_heads.astype(jnp.float32), axis=-1, keepdims=True
    )

    def backward_step(state, key_part, value_part, start):
        count = key_part.shape[0]
        allow = mask_for(start, count)

        def backward_compute(current):
            dq_accum, dk_full, dv_full = current
            key_three = key_part.reshape(count, groups, HEAD_DIM)
            value_three = value_part.reshape(count, groups, HEAD_DIM)
            scores = (
                jnp.einsum("gqd,kgd->gqk", q_heads, key_three, preferred_element_type=jnp.float32)
                * scale_qk
            )
            prob = jnp.where(allow[None], jnp.exp(scores - log_total), 0.0)
            d_prob = jnp.einsum(
                "gqd,kgd->gqk", do_heads, value_three, preferred_element_type=jnp.float32
            )
            d_score = prob * (d_prob - delta)
            prob16 = prob.astype(jnp.bfloat16)
            dscore16 = d_score.astype(jnp.bfloat16)
            dq_accum = dq_accum + scale_qk * jnp.einsum(
                "gqk,kgd->gqd", dscore16, key_three, preferred_element_type=jnp.float32
            )
            dk_part = scale_qk * jnp.einsum(
                "gqk,gqd->kgd", dscore16, q_heads, preferred_element_type=jnp.float32
            )
            dv_part = jnp.einsum(
                "gqk,gqd->kgd", prob16, do_heads, preferred_element_type=jnp.float32
            )
            dk_full = lax.dynamic_update_slice_in_dim(
                dk_full, dk_part.reshape(count, groups * HEAD_DIM), start, 0
            )
            dv_full = lax.dynamic_update_slice_in_dim(
                dv_full, dv_part.reshape(count, groups * HEAD_DIM), start, 0
            )
            return (dq_accum, dk_full, dv_full)

        return lax.cond(jnp.any(allow), backward_compute, lambda current: current, state)

    init_bwd = (
        jnp.zeros((groups, Q_PER_KV * q_count, HEAD_DIM), jnp.float32),
        jnp.zeros((n_keys, groups * HEAD_DIM), jnp.float32),
        jnp.zeros((n_keys, groups * HEAD_DIM), jnp.float32),
    )
    bwd_state = sweep_keys(init_bwd, all_keys, all_values, 0, backward_step)
    dq_accum, dk_full, dv_full = bwd_state
    dq_heads = dq_accum.astype(jnp.bfloat16)
    shards = lax.axis_size("ctx")
    feat = groups * HEAD_DIM
    per_shard = q_count // BLOCK
    doc_most = n_keys // BLOCK // 2 + 3 * per_shard
    reach = min(shards - 1, (doc_most + per_shard - 2) // per_shard)
    partial_key = dk_full.reshape(shards, q_count, feat)
    partial_value = dv_full.reshape(shards, q_count, feat)
    both = jnp.stack((partial_key, partial_value), axis=0)
    padded = jnp.concatenate((jnp.zeros((2, reach, q_count, feat), jnp.float32), both), axis=1)
    window = lax.dynamic_slice_in_dim(padded, lax.axis_index("ctx"), reach + 1, 1)
    buffer = window[:, ::-1]
    top_bit = reach.bit_length() - 1
    for bit in range(top_bit, -1, -1):
        stride = 1 << bit
        movers = np.array([dist for dist in range(reach + 1) if dist & stride], dtype=np.int32)
        landing = movers - stride
        outgoing = buffer[:, movers]
        arrived = passed_along(outgoing.astype(jnp.bfloat16), "ctx", -stride).astype(outgoing.dtype)
        buffer = buffer.at[:, movers].set(0.0)
        buffer = buffer.at[:, landing].add(arrived)
    summed = buffer[:, 0]
    key_grad16 = summed[0].astype(jnp.bfloat16)
    value_grad16 = summed[1].astype(jnp.bfloat16)
    d_key, d_value = (
        lax.all_to_all(key_grad16, "head", split_axis=0, concat_axis=1, tiled=True),
        lax.all_to_all(value_grad16, "head", split_axis=0, concat_axis=1, tiled=True),
    )
    return (rows_first(out_heads), rows_first(dq_heads), d_key, d_value)


def solution(mesh):
    placed = (
        P("ctx", "head"),
        P(("ctx", "head"), None),
        P(("ctx", "head"), None),
        P("ctx", "head"),
        P(),
        P(),
    )
    return jax.shard_map(
        body,
        mesh=mesh,
        in_specs=placed,
        out_specs=(
            P("ctx", "head"),
            P("ctx", "head"),
            P(("ctx", "head"), None),
            P(("ctx", "head"), None),
        ),
        check_vma=False,
    )
```

profile of v0, /device:TPU:6, one launch (start us, length us, event | category | flops | bytes accessed | tf_op | source)
XLA Modules:
  0.0 2207.5 jit_solution(17359374451410437579)
XLA Ops:
  7.9 13.1 all_to_all.70
  21.9 9.3 all_to_all.71
  33.8 71.8 %all-gather.3.cloned.1.call-done = bf16[8192,128]{1,0:T(8,128)(2,1)} async-done(((bf16[128,128]{1,0:T(8,128)(2,1)}), bf16[8192,128]{1,0:T(8,128)(2,1)}) %all-gather.3.cloned.1.call-update) | async-done | bytes 2097168 | tf_op jit(solution)/shard_map/all_gather | solution.py:103
  105.6 83.6 %all-gather.5.cloned.1.call-done = bf16[8192,128]{1,0:T(8,128)(2,1)} async-done(((bf16[128,128]{1,0:T(8,128)(2,1)}), bf16[8192,128]{1,0:T(8,128)(2,1)}) %all-gather.5.cloned.1.call-update) | async-done | bytes 2097168 | tf_op jit(solution)/shard_map/all_gather | solution.py:104
  189.2 872.1 %while.44 = (s32[]{:T(128)}, f32[1,512,1]{1,2,0:T(1,128)S(1)}, f32[1,512,1]{1,2,0:T(1,128)S(1)}, f32[1,512,128]{2,1,0:T(8,128)S(1)}, s32[64,64]{1,0:T(8,128)}, /...) while((s32[]{:T(128)}, f32[1,512,1]{1,2,0:T(1,128)S(1)}, ...), condition=%wide.region_6.11_spmd.clone.clone, body=%wide.region_0.10_spmd.clone.clone.sunk | while | flops 137744896 | bytes 6490953 | solution.py:41
  197.1 40.0 %select_select_fusion.4 = s32[512]{0:T(512)S(1)} fusion(s32[]{:T(128)} %bitcast.437, s32[]{:T(128)} %bitcast.438, s32[]{:T(128)} %bitcast.439, s32[]{:T(128)} %bitcast.440, s32[]{:T(128)} %bitcast.441, s32[]{:T(128)} %bitcast.442, s32[]{:T(128)} %bitcast.443, s32[]{:T(128)} %bitcast.444, s32[]{:T(128)} %bitcast.445, s32[]{:T(128)} %bitcast.446, ...), kind=kLoop, calls=%fused_computation.93.clone.1 | loop fusion | flops 76288 | bytes 2308 | tf_op jit(solution)/shard_map/while/body/eval_jaxpr/jit(_take)/select_n | solution.py:25
  254.7 40.0 %select_select_fusion.4 = s32[512]{0:T(512)S(1)} fusion(s32[]{:T(128)} %bitcast.437, s32[]{:T(128)} %bitcast.438, s32[]{:T(128)} %bitcast.439, s32[]{:T(128)} %bitcast.440, s32[]{:T(128)} %bitcast.441, s32[]{:T(128)} %bitcast.442, s32[]{:T(128)} %bitcast.443, s32[]{:T(128)} %bitcast.444, s32[]{:T(128)} %bitcast.445, s32[]{:T(128)} %bitcast.446, ...), kind=kLoop, calls=%fused_computation.93.clone.1 | loop fusion | flops 76288 | bytes 2308 | tf_op jit(solution)/shard_map/while/body/eval_jaxpr/jit(_take)/select_n | solution.py:25
  309.0 40.0 %select_select_fusion.4 = s32[512]{0:T(512)S(1)} fusion(s32[]{:T(128)} %bitcast.437, s32[]{:T(128)} %bitcast.438, s32[]{:T(128)} %bitcast.439, s32[]{:T(128)} %bitcast.440, s32[]{:T(128)} %bitcast.441, s32[]{:T(128)} %bitcast.442, s32[]{:T(128)} %bitcast.443, s32[]{:T(128)} %bitcast.444, s32[]{:T(128)} %bitcast.445, s32[]{:T(128)} %bitcast.446, ...), kind=kLoop, calls=%fused_computation.93.clone.1 | loop fusion | flops 76288 | bytes 2308 | tf_op jit(solution)/shard_map/while/body/eval_jaxpr/jit(_take)/select_n | solution.py:25
  363.3 40.0 %select_select_fusion.4 = s32[512]{0:T(512)S(1)} fusion(s32[]{:T(128)} %bitcast.437, s32[]{:T(128)} %bitcast.438, s32[]{:T(128)} %bitcast.439, s32[]{:T(128)} %bitcast.440, s32[]{:T(128)} %bitcast.441, s32[]{:T(128)} %bitcast.442, s32[]{:T(128)} %bitcast.443, s32[]{:T(128)} %bitcast.444, s32[]{:T(128)} %bitcast.445, s32[]{:T(128)} %bitcast.446, ...), kind=kLoop, calls=%fused_computation.93.clone.1 | loop fusion | flops 76288 | bytes 2308 | tf_op jit(solution)/shard_map/while/body/eval_jaxpr/jit(_take)/select_n | solution.py:25
  417.6 40.0 %select_select_fusion.4 = s32[512]{0:T(512)S(1)} fusion(s32[]{:T(128)} %bitcast.437, s32[]{:T(128)} %bitcast.438, s32[]{:T(128)} %bitcast.439, s32[]{:T(128)} %bitcast.440, s32[]{:T(128)} %bitcast.441, s32[]{:T(128)} %bitcast.442, s32[]{:T(128)} %bitcast.443, s32[]{:T(128)} %bitcast.444, s32[]{:T(128)} %bitcast.445, s32[]{:T(128)} %bitcast.446, ...), kind=kLoop, calls=%fused_computation.93.clone.1 | loop fusion | flops 76288 | bytes 2308 | tf_op jit(solution)/shard_map/while/body/eval_jaxpr/jit(_take)/select_n | solution.py:25
  471.9 40.0 %select_select_fusion.4 = s32[512]{0:T(512)S(1)} fusion(s32[]{:T(128)} %bitcast.437, s32[]{:T(128)} %bitcast.438, s32[]{:T(128)} %bitcast.439, s32[]{:T(128)} %bitcast.440, s32[]{:T(128)} %bitcast.441, s32[]{:T(128)} %bitcast.442, s32[]{:T(128)} %bitcast.443, s32[]{:T(128)} %bitcast.444, s32[]{:T(128)} %bitcast.445, s32[]{:T(128)} %bitcast.446, ...), kind=kLoop, calls=%fused_computation.93.clone.1 | loop fusion | flops 76288 | bytes 2308 | tf_op jit(solution)/shard_map/while/body/eval_jaxpr/jit(_take)/select_n | solution.py:25
  526.2 40.0 %select_select_fusion.4 = s32[512]{0:T(512)S(1)} fusion(s32[]{:T(128)} %bitcast.437, s32[]{:T(128)} %bitcast.438, s32[]{:T(128)} %bitcast.439, s32[]{:T(128)} %bitcast.440, s32[]{:T(128)} %bitcast.441, s32[]{:T(128)} %bitcast.442, s32[]{:T(128)} %bitcast.443, s32[]{:T(128)} %bitcast.444, s32[]{:T(128)} %bitcast.445, s32[]{:T(128)} %bitcast.446, ...), kind=kLoop, calls=%fused_computation.93.clone.1 | loop fusion | flops 76288 | bytes 2308 | tf_op jit(solution)/shard_map/while/body/eval_jaxpr/jit(_take)/select_n | solution.py:25
  580.5 40.0 %select_select_fusion.4 = s32[512]{0:T(512)S(1)} fusion(s32[]{:T(128)} %bitcast.437, s32[]{:T(128)} %bitcast.438, s32[]{:T(128)} %bitcast.439, s32[]{:T(128)} %bitcast.440, s32[]{:T(128)} %bitcast.441, s32[]{:T(128)} %bitcast.442, s32[]{:T(128)} %bitcast.443, s32[]{:T(128)} %bitcast.444, s32[]{:T(128)} %bitcast.445, s32[]{:T(128)} %bitcast.446, ...), kind=kLoop, calls=%fused_computation.93.clone.1 | loop fusion | flops 76288 | bytes 2308 | tf_op jit(solution)/shard_map/while/body/eval_jaxpr/jit(_take)/select_n | solution.py:25
  634.8 40.0 %select_select_fusion.4 = s32[512]{0:T(512)S(1)} fusion(s32[]{:T(128)} %bitcast.437, s32[]{:T(128)} %bitcast.438, s32[]{:T(128)} %bitcast.439, s32[]{:T(128)} %bitcast.440, s32[]{:T(128)} %bitcast.441, s32[]{:T(128)} %bitcast.442, s32[]{:T(128)} %bitcast.443, s32[]{:T(128)} %bitcast.444, s32[]{:T(128)} %bitcast.445, s32[]{:T(128)} %bitcast.446, ...), kind=kLoop, calls=%fused_computation.93.clone.1 | loop fusion | flops 76288 | bytes 2308 | tf_op jit(solution)/shard_map/while/body/eval_jaxpr/jit(_take)/select_n | solution.py:25
  689.1 40.0 %select_select_fusion.4 = s32[512]{0:T(512)S(1)} fusion(s32[]{:T(128)} %bitcast.437, s32[]{:T(128)} %bitcast.438, s32[]{:T(128)} %bitcast.439, s32[]{:T(128)} %bitcast.440, s32[]{:T(128)} %bitcast.441, s32[]{:T(128)} %bitcast.442, s32[]{:T(128)} %bitcast.443, s32[]{:T(128)} %bitcast.444, s32[]{:T(128)} %bitcast.445, s32[]{:T(128)} %bitcast.446, ...), kind=kLoop, calls=%fused_computation.93.clone.1 | loop fusion | flops 76288 | bytes 2308 | tf_op jit(solution)/shard_map/while/body/eval_jaxpr/jit(_take)/select_n | solution.py:25
  743.4 40.0 %select_select_fusion.4 = s32[512]{0:T(512)S(1)} fusion(s32[]{:T(128)} %bitcast.437, s32[]{:T(128)} %bitcast.438, s32[]{:T(128)} %bitcast.439, s32[]{:T(128)} %bitcast.440, s32[]{:T(128)} %bitcast.441, s32[]{:T(128)} %bitcast.442, s32[]{:T(128)} %bitcast.443, s32[]{:T(128)} %bitcast.444, s32[]{:T(128)} %bitcast.445, s32[]{:T(128)} %bitcast.446, ...), kind=kLoop, calls=%fused_computation.93.clone.1 | loop fusion | flops 76288 | bytes 2308 | tf_op jit(solution)/shard_map/while/body/eval_jaxpr/jit(_take)/select_n | solution.py:25
  797.6 40.0 %select_select_fusion.4 = s32[512]{0:T(512)S(1)} fusion(s32[]{:T(128)} %bitcast.437, s32[]{:T(128)} %bitcast.438, s32[]{:T(128)} %bitcast.439, s32[]{:T(128)} %bitcast.440, s32[]{:T(128)} %bitcast.441, s32[]{:T(128)} %bitcast.442, s32[]{:T(128)} %bitcast.443, s32[]{:T(128)} %bitcast.444, s32[]{:T(128)} %bitcast.445, s32[]{:T(128)} %bitcast.446, ...), kind=kLoop, calls=%fused_computation.93.clone.1 | loop fusion | flops 76288 | bytes 2308 | tf_op jit(solution)/shard_map/while/body/eval_jaxpr/jit(_take)/select_n | solution.py:25
  851.9 40.0 %select_select_fusion.4 = s32[512]{0:T(512)S(1)} fusion(s32[]{:T(128)} %bitcast.437, s32[]{:T(128)} %bitcast.438, s32[]{:T(128)} %bitcast.439, s32[]{:T(128)} %bitcast.440, s32[]{:T(128)} %bitcast.441, s32[]{:T(128)} %bitcast.442, s32[]{:T(128)} %bitcast.443, s32[]{:T(128)} %bitcast.444, s32[]{:T(128)} %bitcast.445, s32[]{:T(128)} %bitcast.446, ...), kind=kLoop, calls=%fused_computation.93.clone.1 | loop fusion | flops 76288 | bytes 2308 | tf_op jit(solution)/shard_map/while/body/eval_jaxpr/jit(_take)/select_n | solution.py:25
  906.2 40.0 %select_select_fusion.4 = s32[512]{0:T(512)S(1)} fusion(s32[]{:T(128)} %bitcast.437, s32[]{:T(128)} %bitcast.438, s32[]{:T(128)} %bitcast.439, s32[]{:T(128)} %bitcast.440, s32[]{:T(128)} %bitcast.441, s32[]{:T(128)} %bitcast.442, s32[]{:T(128)} %bitcast.443, s32[]{:T(128)} %bitcast.444, s32[]{:T(128)} %bitcast.445, s32[]{:T(128)} %bitcast.446, ...), kind=kLoop, calls=%fused_computation.93.clone.1 | loop fusion | flops 76288 | bytes 2308 | tf_op jit(solution)/shard_map/while/body/eval_jaxpr/jit(_take)/select_n | solution.py:25
  960.5 40.0 %select_select_fusion.4 = s32[512]{0:T(512)S(1)} fusion(s32[]{:T(128)} %bitcast.437, s32[]{:T(128)} %bitcast.438, s32[]{:T(128)} %bitcast.439, s32[]{:T(128)} %bitcast.440, s32[]{:T(128)} %bitcast.441, s32[]{:T(128)} %bitcast.442, s32[]{:T(128)} %bitcast.443, s32[]{:T(128)} %bitcast.444, s32[]{:T(128)} %bitcast.445, s32[]{:T(128)} %bitcast.446, ...), kind=kLoop, calls=%fused_computation.93.clone.1 | loop fusion | flops 76288 | bytes 2308 | tf_op jit(solution)/shard_map/while/body/eval_jaxpr/jit(_take)/select_n | solution.py:25
  1014.8 40.0 %select_select_fusion.4 = s32[512]{0:T(512)S(1)} fusion(s32[]{:T(128)} %bitcast.437, s32[]{:T(128)} %bitcast.438, s32[]{:T(128)} %bitcast.439, s32[]{:T(128)} %bitcast.440, s32[]{:T(128)} %bitcast.441, s32[]{:T(128)} %bitcast.442, s32[]{:T(128)} %bitcast.443, s32[]{:T(128)} %bitcast.444, s32[]{:T(128)} %bitcast.445, s32[]{:T(128)} %bitcast.446, ...), kind=kLoop, calls=%fused_computation.93.clone.1 | loop fusion | flops 76288 | bytes 2308 | tf_op jit(solution)/shard_map/while/body/eval_jaxpr/jit(_take)/select_n | solution.py:25
  1066.2 769.5 %while.45 = (s32[]{:T(128)}, f32[1,512,128]{2,1,0:T(8,128)S(1)}, f32[8192,128]{1,0:T(8,128)}, f32[8192,128]{1,0:T(8,128)}, s32[64,64]{1,0:T(8,128)S(1)}, /*index...) while((s32[]{:T(128)}, f32[1,512,128]{2,1,0:T(8,128)S(1)}, ...), condition=%wide.region_12.17_spmd.clone.clone, body=%wide.region_8.0_spmd.clone.clone.sunk | while | flops 338611712 | bytes 8559493 | solution.py:41
  1069.1 39.5 %select_select_fusion.5 = s32[512]{0:T(512)S(1)} fusion(s32[]{:T(128)} %bitcast.502, s32[]{:T(128)} %bitcast.503, s32[]{:T(128)} %bitcast.504, s32[]{:T(128)} %bitcast.505, s32[]{:T(128)} %bitcast.506, s32[]{:T(128)} %bitcast.507, s32[]{:T(128)} %bitcast.508, s32[]{:T(128)} %bitcast.509, s32[]{:T(128)} %bitcast.510, s32[]{:T(128)} %bitcast.511, ...), kind=kLoop, calls=%fused_computation.127.clone.1 | loop fusion | flops 76288 | bytes 2308 | tf_op jit(solution)/shard_map/while/body/eval_jaxpr/jit(_take)/select_n | solution.py:25
  1113.9 6.1 conditional.9
  1122.9 39.5 %select_select_fusion.5 = s32[512]{0:T(512)S(1)} fusion(s32[]{:T(128)} %bitcast.502, s32[]{:T(128)} %bitcast.503, s32[]{:T(128)} %bitcast.504, s32[]{:T(128)} %bitcast.505, s32[]{:T(128)} %bitcast.506, s32[]{:T(128)} %bitcast.507, s32[]{:T(128)} %bitcast.508, s32[]{:T(128)} %bitcast.509, s32[]{:T(128)} %bitcast.510, s32[]{:T(128)} %bitcast.511, ...), kind=kLoop, calls=%fused_computation.127.clone.1 | loop fusion | flops 76288 | bytes 2308 | tf_op jit(solution)/shard_map/while/body/eval_jaxpr/jit(_take)/select_n | solution.py:25
  1170.6 39.5 %select_select_fusion.5 = s32[512]{0:T(512)S(1)} fusion(s32[]{:T(128)} %bitcast.502, s32[]{:T(128)} %bitcast.503, s32[]{:T(128)} %bitcast.504, s32[]{:T(128)} %bitcast.505, s32[]{:T(128)} %bitcast.506, s32[]{:T(128)} %bitcast.507, s32[]{:T(128)} %bitcast.508, s32[]{:T(128)} %bitcast.509, s32[]{:T(128)} %bitcast.510, s32[]{:T(128)} %bitcast.511, ...), kind=kLoop, calls=%fused_computation.127.clone.1 | loop fusion | flops 76288 | bytes 2308 | tf_op jit(solution)/shard_map/while/body/eval_jaxpr/jit(_take)/select_n | solution.py:25
  1218.3 39.5 %select_select_fusion.5 = s32[512]{0:T(512)S(1)} fusion(s32[]{:T(128)} %bitcast.502, s32[]{:T(128)} %bitcast.503, s32[]{:T(128)} %bitcast.504, s32[]{:T(128)} %bitcast.505, s32[]{:T(128)} %bitcast.506, s32[]{:T(128)} %bitcast.507, s32[]{:T(128)} %bitcast.508, s32[]{:T(128)} %bitcast.509, s32[]{:T(128)} %bitcast.510, s32[]{:T(128)} %bitcast.511, ...), kind=kLoop, calls=%fused_computation.127.clone.1 | loop fusion | flops 76288 | bytes 2308 | tf_op jit(solution)/shard_map/while/body/eval_jaxpr/jit(_take)/select_n | solution.py:25
  1266.0 39.5 %select_select_fusion.5 = s32[512]{0:T(512)S(1)} fusion(s32[]{:T(128)} %bitcast.502, s32[]{:T(128)} %bitcast.503, s32[]{:T(128)} %bitcast.504, s32[]{:T(128)} %bitcast.505, s32[]{:T(128)} %bitcast.506, s32[]{:T(128)} %bitcast.507, s32[]{:T(128)} %bitcast.508, s32[]{:T(128)} %bitcast.509, s32[]{:T(128)} %bitcast.510, s32[]{:T(128)} %bitcast.511, ...), kind=kLoop, calls=%fused_computation.127.clone.1 | loop fusion | flops 76288 | bytes 2308 | tf_op jit(solution)/shard_map/while/body/eval_jaxpr/jit(_take)/select_n | solution.py:25
  1313.7 39.5 %select_select_fusion.5 = s32[512]{0:T(512)S(1)} fusion(s32[]{:T(128)} %bitcast.502, s32[]{:T(128)} %bitcast.503, s32[]{:T(128)} %bitcast.504, s32[]{:T(128)} %bitcast.505, s32[]{:T(128)} %bitcast.506, s32[]{:T(128)} %bitcast.507, s32[]{:T(128)} %bitcast.508, s32[]{:T(128)} %bitcast.509, s32[]{:T(128)} %bitcast.510, s32[]{:T(128)} %bitcast.511, ...), kind=kLoop, calls=%fused_computation.127.clone.1 | loop fusion | flops 76288 | bytes 2308 | tf_op jit(solution)/shard_map/while/body/eval_jaxpr/jit(_take)/select_n | solution.py:25
  1361.4 39.5 %select_select_fusion.5 = s32[512]{0:T(512)S(1)} fusion(s32[]{:T(128)} %bitcast.502, s32[]{:T(128)} %bitcast.503, s32[]{:T(128)} %bitcast.504, s32[]{:T(128)} %bitcast.505, s32[]{:T(128)} %bitcast.506, s32[]{:T(128)} %bitcast.507, s32[]{:T(128)} %bitcast.508, s32[]{:T(128)} %bitcast.509, s32[]{:T(128)} %bitcast.510, s32[]{:T(128)} %bitcast.511, ...), kind=kLoop, calls=%fused_computation.127.clone.1 | loop fusion | flops 76288 | bytes 2308 | tf_op jit(solution)/shard_map/while/body/eval_jaxpr/jit(_take)/select_n | solution.py:25
  1409.2 39.5 %select_select_fusion.5 = s32[512]{0:T(512)S(1)} fusion(s32[]{:T(128)} %bitcast.502, s32[]{:T(128)} %bitcast.503, s32[]{:T(128)} %bitcast.504, s32[]{:T(128)} %bitcast.505, s32[]{:T(128)} %bitcast.506, s32[]{:T(128)} %bitcast.507, s32[]{:T(128)} %bitcast.508, s32[]{:T(128)} %bitcast.509, s32[]{:T(128)} %bitcast.510, s32[]{:T(128)} %bitcast.511, ...), kind=kLoop, calls=%fused_computation.127.clone.1 | loop fusion | flops 76288 | bytes 2308 | tf_op jit(solution)/shard_map/while/body/eval_jaxpr/jit(_take)/select_n | solution.py:25
  1456.9 39.5 %select_select_fusion.5 = s32[512]{0:T(512)S(1)} fusion(s32[]{:T(128)} %bitcast.502, s32[]{:T(128)} %bitcast.503, s32[]{:T(128)} %bitcast.504, s32[]{:T(128)} %bitcast.505, s32[]{:T(128)} %bitcast.506, s32[]{:T(128)} %bitcast.507, s32[]{:T(128)} %bitcast.508, s32[]{:T(128)} %bitcast.509, s32[]{:T(128)} %bitcast.510, s32[]{:T(128)} %bitcast.511, ...), kind=kLoop, calls=%fused_computation.127.clone.1 | loop fusion | flops 76288 | bytes 2308 | tf_op jit(solution)/shard_map/while/body/eval_jaxpr/jit(_take)/select_n | solution.py:25
  1504.6 39.5 %select_select_fusion.5 = s32[512]{0:T(512)S(1)} fusion(s32[]{:T(128)} %bitcast.502, s32[]{:T(128)} %bitcast.503, s32[]{:T(128)} %bitcast.504, s32[]{:T(128)} %bitcast.505, s32[]{:T(128)} %bitcast.506, s32[]{:T(128)} %bitcast.507, s32[]{:T(128)} %bitcast.508, s32[]{:T(128)} %bitcast.509, s32[]{:T(128)} %bitcast.510, s32[]{:T(128)} %bitcast.511, ...), kind=kLoop, calls=%fused_computation.127.clone.1 | loop fusion | flops 76288 | bytes 2308 | tf_op jit(solution)/shard_map/while/body/eval_jaxpr/jit(_take)/select_n | solution.py:25
  1552.3 39.5 %select_select_fusion.5 = s32[512]{0:T(512)S(1)} fusion(s32[]{:T(128)} %bitcast.502, s32[]{:T(128)} %bitcast.503, s32[]{:T(128)} %bitcast.504, s32[]{:T(128)} %bitcast.505, s32[]{:T(128)} %bitcast.506, s32[]{:T(128)} %bitcast.507, s32[]{:T(128)} %bitcast.508, s32[]{:T(128)} %bitcast.509, s32[]{:T(128)} %bitcast.510, s32[]{:T(128)} %bitcast.511, ...), kind=kLoop, calls=%fused_computation.127.clone.1 | loop fusion | flops 76288 | bytes 2308 | tf_op jit(solution)/shard_map/while/body/eval_jaxpr/jit(_take)/select_n | solution.py:25
  1600.0 39.5 %select_select_fusion.5 = s32[512]{0:T(512)S(1)} fusion(s32[]{:T(128)} %bitcast.502, s32[]{:T(128)} %bitcast.503, s32[]{:T(128)} %bitcast.504, s32[]{:T(128)} %bitcast.505, s32[]{:T(128)} %bitcast.506, s32[]{:T(128)} %bitcast.507, s32[]{:T(128)} %bitcast.508, s32[]{:T(128)} %bitcast.509, s32[]{:T(128)} %bitcast.510, s32[]{:T(128)} %bitcast.511, ...), kind=kLoop, calls=%fused_computation.127.clone.1 | loop fusion | flops 76288 | bytes 2308 | tf_op jit(solution)/shard_map/while/body/eval_jaxpr/jit(_take)/select_n | solution.py:25
  1647.7 39.5 %select_select_fusion.5 = s32[512]{0:T(512)S(1)} fusion(s32[]{:T(128)} %bitcast.502, s32[]{:T(128)} %bitcast.503, s32[]{:T(128)} %bitcast.504, s32[]{:T(128)} %bitcast.505, s32[]{:T(128)} %bitcast.506, s32[]{:T(128)} %bitcast.507, s32[]{:T(128)} %bitcast.508, s32[]{:T(128)} %bitcast.509, s32[]{:T(128)} %bitcast.510, s32[]{:T(128)} %bitcast.511, ...), kind=kLoop, calls=%fused_computation.127.clone.1 | loop fusion | flops 76288 | bytes 2308 | tf_op jit(solution)/shard_map/while/body/eval_jaxpr/jit(_take)/select_n | solution.py:25
  1695.4 39.5 %select_select_fusion.5 = s32[512]{0:T(512)S(1)} fusion(s32[]{:T(128)} %bitcast.502, s32[]{:T(128)} %bitcast.503, s32[]{:T(128)} %bitcast.504, s32[]{:T(128)} %bitcast.505, s32[]{:T(128)} %bitcast.506, s32[]{:T(128)} %bitcast.507, s32[]{:T(128)} %bitcast.508, s32[]{:T(128)} %bitcast.509, s32[]{:T(128)} %bitcast.510, s32[]{:T(128)} %bitcast.511, ...), kind=kLoop, calls=%fused_computation.127.clone.1 | loop fusion | flops 76288 | bytes 2308 | tf_op jit(solution)/shard_map/while/body/eval_jaxpr/jit(_take)/select_n | solution.py:25
  1743.2 39.5 %select_select_fusion.5 = s32[512]{0:T(512)S(1)} fusion(s32[]{:T(128)} %bitcast.502, s32[]{:T(128)} %bitcast.503, s32[]{:T(128)} %bitcast.504, s32[]{:T(128)} %bitcast.505, s32[]{:T(128)} %bitcast.506, s32[]{:T(128)} %bitcast.507, s32[]{:T(128)} %bitcast.508, s32[]{:T(128)} %bitcast.509, s32[]{:T(128)} %bitcast.510, s32[]{:T(128)} %bitcast.511, ...), kind=kLoop, calls=%fused_computation.127.clone.1 | loop fusion | flops 76288 | bytes 2308 | tf_op jit(solution)/shard_map/while/body/eval_jaxpr/jit(_take)/select_n | solution.py:25
  1790.9 39.5 %select_select_fusion.5 = s32[512]{0:T(512)S(1)} fusion(s32[]{:T(128)} %bitcast.502, s32[]{:T(128)} %bitcast.503, s32[]{:T(128)} %bitcast.504, s32[]{:T(128)} %bitcast.505, s32[]{:T(128)} %bitcast.506, s32[]{:T(128)} %bitcast.507, s32[]{:T(128)} %bitcast.508, s32[]{:T(128)} %bitcast.509, s32[]{:T(128)} %bitcast.510, s32[]{:T(128)} %bitcast.511, ...), kind=kLoop, calls=%fused_computation.127.clone.1 | loop fusion | flops 76288 | bytes 2308 | tf_op jit(solution)/shard_map/while/body/eval_jaxpr/jit(_take)/select_n | solution.py:25
  1851.5 16.6 collective-permute-done
  1880.2 58.8 %collective-permute-done.1 = bf16[2,16,128,128]{3,2,0,1:T(8,128)(2,1)} collective-permute-done((bf16[2,16,128,128]{3,2,0,1:T(8,128)(2,1)}, bf16[2,16,128,128]{3,2,0,1:T(8,128)(2,1)}, u32[]{:S(2)}, u32[]{:S(2)}) %collective-permute-start.1) | collective-permute-done | bytes 1048608 | tf_op jit(solution)/shard_map/ppermute | solution.py:18
  1956.1 50.8 %collective-permute-done.2 = bf16[2,16,128,128]{3,2,0,1:T(8,128)(2,1)} collective-permute-done((bf16[2,16,128,128]{3,2,0,1:T(8,128)(2,1)}, bf16[2,16,128,128]{3,2,0,1:T(8,128)(2,1)}, u32[]{:S(2)}, u32[]{:S(2)}) %collective-permute-start.2) | collective-permute-done | bytes 1048608 | tf_op jit(solution)/shard_map/ppermute | solution.py:18
  2024.2 32.3 %collective-permute-done.3 = bf16[2,16,128,128]{3,2,0,1:T(8,128)(2,1)} collective-permute-done((bf16[2,16,128,128]{3,2,0,1:T(8,128)(2,1)}, bf16[2,16,128,128]{3,2,0,1:T(8,128)(2,1)}, u32[]{:S(2)}, u32[]{:S(2)}) %collective-permute-start.3) | collective-permute-done | bytes 1048608 | tf_op jit(solution)/shard_map/ppermute | solution.py:18
  2068.2 7.7 scatter_fusion.8
  2075.9 64.9 %collective-permute-done.4 = bf16[2,17,128,128]{3,2,0,1:T(8,128)(2,1)} collective-permute-done((bf16[2,17,128,128]{3,2,0,1:T(8,128)(2,1)}, bf16[2,17,128,128]{3,2,0,1:T(8,128)(2,1)}, u32[]{:S(2)}, u32[]{:S(2)}) %collective-permute-start.4) | collective-permute-done | bytes 1114144 | tf_op jit(solution)/shard_map/ppermute | solution.py:18
  2143.7 10.1 scatter_fusion.9
  2159.7 7.5 scatter_fusion.10
  2168.7 9.5 scatter_fusion.11
  (811 shorter events, 463.2 us)
Async XLA Ops:
  7.2 0.8 copy-start
  7.2 98.4 %all-gather.3.cloned.1.call-start = ((), (), s32[]{:S(2)}) async-start(), calls=%async_computation.4 | async-start | bytes 2129920 | tf_op jit(solution)/shard_map/all_gather | solution.py:103
  21.0 168.1 %all-gather.5.cloned.1.call-start = ((), (), s32[]{:S(2)}) async-start(), calls=%async_computation.5 | async-start | bytes 2129920 | tf_op jit(solution)/shard_map/all_gather | solution.py:104
  1061.6 4.6 copy-start.1
  1061.6 4.6 copy-start.2
  1839.8 9.2 copy-start.5
  1839.8 9.3 copy-start.6
  1844.8 31.3 %copy-start.4 = (s32[16]{0:T(128)S(1)}, s32[16]{0:T(128)}, u32[]{:S(2)}) copy-start(s32[16]{0:T(128)} %constant.541) | copy-start | bytes 196
  1847.7 20.5 collective-permute-start
  1874.7 64.3 %collective-permute-start.1 = (bf16[2,16,128,128]{3,2,0,1:T(8,128)(2,1)}, bf16[2,16,128,128]{3,2,0,1:T(8,128)(2,1)}, u32[]{:S(2)}, u32[]{:S(2)}) collective-permute-start(bf16[2,16,128,128]{3,2,0,1:T(8,128)(2,1)} %bitcast.292), channel_id=1, source_target_pairs={{128,0},{136,8},{144,16},{152,24},{160,32},{168,40},{176,48},{184,... | collective-permute-start | bytes 3145736 | tf_op jit(solution)/shard_map/ppermute | solution.py:18
  1941.8 10.6 copy-start.3
  1951.0 55.9 %collective-permute-start.2 = (bf16[2,16,128,128]{3,2,0,1:T(8,128)(2,1)}, bf16[2,16,128,128]{3,2,0,1:T(8,128)(2,1)}, u32[]{:S(2)}, u32[]{:S(2)}) collective-permute-start(bf16[2,16,128,128]{3,2,0,1:T(8,128)(2,1)} %bitcast.576), channel_id=1, source_target_pairs={{64,0},{72,8},{80,16},{88,24},{96,32},{104,40},{112,48},{120,56},{... | collective-permute-start | bytes 3145736 | tf_op jit(solution)/shard_map/ppermute | solution.py:18
  1952.3 57.4 %copy-start.10 = (s32[16]{0:T(128)S(1)}, s32[16]{0:T(128)}, u32[]{:S(2)}) copy-start(s32[16]{0:T(128)} %constant.542) | copy-start | bytes 196
  2009.8 10.6 copy-start.8
  2019.1 37.4 %collective-permute-start.3 = (bf16[2,16,128,128]{3,2,0,1:T(8,128)(2,1)}, bf16[2,16,128,128]{3,2,0,1:T(8,128)(2,1)}, u32[]{:S(2)}, u32[]{:S(2)}) collective-permute-start(bf16[2,16,128,128]{3,2,0,1:T(8,128)(2,1)} %bitcast.575), channel_id=1, source_target_pairs={{32,0},{40,8},{48,16},{56,24},{64,32},{72,40},{80,48},{88,56},{96,... | collective-permute-start | bytes 3145736 | tf_op jit(solution)/shard_map/ppermute | solution.py:18
  2020.4 37.5 %copy-start.9 = (s32[16]{0:T(128)S(1)}, s32[16]{0:T(128)}, u32[]{:S(2)}) copy-start(s32[16]{0:T(128)} %constant.545) | copy-start | bytes 196
  2058.0 10.0 copy-start.7
  2066.7 74.2 %collective-permute-start.4 = (bf16[2,17,128,128]{3,2,0,1:T(8,128)(2,1)}, bf16[2,17,128,128]{3,2,0,1:T(8,128)(2,1)}, u32[]{:S(2)}, u32[]{:S(2)}) collective-permute-start(bf16[2,17,128,128]{3,2,0,1:T(8,128)(2,1)} %bitcast.289), channel_id=1, source_target_pairs={{16,0},{24,8},{32,16},{40,24},{48,32},{56,40},{64,48},{72,56},{80,... | collective-permute-start | bytes 3342344 | tf_op jit(solution)/shard_map/ppermute | solution.py:18
  2068.2 75.5 %copy-start.11 = (s32[17]{0:T(128)S(1)}, s32[17]{0:T(128)}, u32[]{:S(2)}) copy-start(s32[17]{0:T(128)} %constant.548) | copy-start | bytes 208
  2157.9 9.3 collective-permute-start.5
  2181.5 9.0 all-to-all-start.3
  2190.5 9.5 all-to-all-start.2
Sparse Core Ops, SparseCore 0:
  21.2 84.3 all-gather.2
  108.9 80.2 all-gather.4
where the time goes:
time: 2250 us; the launch traced here: 2210 us
  other arithmetic  1380 us (61%)
  waiting for transfers between devices  386 us (17%)
  local copies, waits for them, and re-layouts  357 us (16%)
  loops' own time  25.1 us (1%)
    select_n x32, other arithmetic, allowed_pairs(): jnp.take(block_doc, k_blk)[None, :]  1270 us
    ppermute x6, waiting for transfers between devices, passed_along(): return lax.ppermute(block, axis, route)  224 us
    gather x128, local copies, waits for them, and re-layouts, allowed_pairs(): jnp.take(block_doc, k_blk)[None, :]  171 us
    all_gather x1, waiting for transfers between devices, body(): lax.all_gather(values, 'ctx', axis=0, tiled=True)  83.6 us
    all_gather x1, waiting for transfers between devices, body(): lax.all_gather(keys, 'ctx', axis=0, tiled=True)  71.8 us
    gather x64, local copies, waits for them, and re-layouts, allowed_pairs(): table = jnp.take(jnp.take(block_mask, q_blk, axis=0), k_blk, axis=1)  66 us
  transfers between devices with their start and end apart: 10, of which 9 were waited for; matrix products, arithmetic and copies ran while one was open for 2% of the time, Pallas kernels for 0%

commit v1 on v0

v1 whole, which is shorter than its diff:
```python
import jax
import jax.numpy as jnp
import numpy as np
from jax import lax
from jax.experimental import pallas as pl
from jax.experimental.pallas import tpu as pltpu
from jax.sharding import Mesh
from jax.sharding import PartitionSpec as P

HEAD_DIM = 128
Q_PER_KV = 4
BLOCK = 128
PLANE = 8
ZN = 8
SLOTS = 6
ROWS = Q_PER_KV * BLOCK
SCALE = HEAD_DIM**-0.5
LOG2_SCALE = SCALE * float(np.log2(np.e))
LOW = -1e30
FAR = 2e30

PLANE_AXES = ("y", "c")
HEAD_AXES = ("yl", "x")


def dot_nt(a, b):
    return lax.dot_general(a, b, (((1,), (1,)), ((), ())), preferred_element_type=jnp.float32)


def dot_nn(a, b):
    return lax.dot_general(a, b, (((1,), (0,)), ((), ())), preferred_element_type=jnp.float32)


def rows_of(block):
    return jnp.concatenate([block[:, j * HEAD_DIM : (j + 1) * HEAD_DIM] for j in range(Q_PER_KV)], axis=0)


def penalties(pos, doc, mask, b):
    z, a = pos[0], pos[1]
    q_blk = PLANE * z + b
    oks = []
    for s in range(SLOTS):
        kz = z - (SLOTS - 1) + s
        k_blk = jnp.maximum(PLANE * kz + a, 0)
        seen = (k_blk < q_blk) & (mask[q_blk, k_blk] == 1) & (doc[q_blk] == doc[k_blk])
        oks.append((kz >= 0) & (seen | (k_blk == q_blk)))
    return oks


def key_slot(pos, s):
    return jnp.maximum(pos[0] - (SLOTS - 1) + s, 0)


def diagonal_cut(scores, on_diagonal):
    k_at = lax.broadcasted_iota(jnp.int32, (BLOCK, ROWS), 0)
    q_at = lax.broadcasted_iota(jnp.int32, (BLOCK, ROWS), 1) & (BLOCK - 1)
    return jnp.where((k_at <= q_at) | jnp.logical_not(on_diagonal), scores, LOW)


def stats_kernel(pos, doc, mask, qd_ref, kv_ref, st_ref):
    b = pl.program_id(0)
    oks = penalties(pos, doc, mask, b)
    q = rows_of(qd_ref[0, 0])
    do = rows_of(qd_ref[0, 1])
    scores = []
    top = jnp.full((1, ROWS), LOW, jnp.float32)
    for s in range(SLOTS):
        k = kv_ref[key_slot(pos, s), :, :HEAD_DIM]
        sc = dot_nt(k, q)
        if s == SLOTS - 1:
            sc = diagonal_cut(sc, pos[1] == b)
        scores.append(sc)
        most = jnp.max(sc, axis=0, keepdims=True) * LOG2_SCALE
        top = jnp.maximum(top, jnp.where(oks[s], most, LOW))
    total = jnp.zeros((1, ROWS), jnp.float32)
    inner = jnp.zeros((1, ROWS), jnp.float32)
    for s in range(SLOTS):
        v = kv_ref[key_slot(pos, s), :, HEAD_DIM:]
        w = jnp.exp2(scores[s] * LOG2_SCALE - (top + jnp.where(oks[s], 0.0, FAR)))
        dp = dot_nt(v, do)
        total += jnp.sum(w, axis=0, keepdims=True)
        inner += jnp.sum(w * dp, axis=0, keepdims=True)
    st_ref[0, pl.ds(b, 1), :] = jnp.where(total > 0.0, top + jnp.log2(jnp.maximum(total, 1.0)), LOW)
    st_ref[1, pl.ds(b, 1), :] = inner / jnp.maximum(total, 1.0)


def grads_kernel(pos, doc, mask, st_ref, qd_ref, kv_ref, od_ref, dkv_ref, kt, vt, dk, dv, p16, ds16):
    b = pl.program_id(0)

    @pl.when(b == 0)
    def _():
        dk[...] = jnp.zeros_like(dk)
        dv[...] = jnp.zeros_like(dv)
        for s in range(SLOTS):
            both = kv_ref[key_slot(pos, s)]
            kt[:, s * BLOCK : (s + 1) * BLOCK] = both[:, :HEAD_DIM].T
            vt[:, s * BLOCK : (s + 1) * BLOCK] = both[:, HEAD_DIM:].T

    lse_parts = st_ref[:, 0, pl.ds(b, 1), :]
    delta_parts = st_ref[:, 1, pl.ds(b, 1), :]
    most = jnp.max(lse_parts, axis=0)
    lse = most + jnp.log2(jnp.sum(jnp.exp2(lse_parts - most[None]), axis=0))
    delta = jnp.sum(jnp.exp2(lse_parts - lse[None]) * delta_parts, axis=0)

    oks = penalties(pos, doc, mask, b)
    q = rows_of(qd_ref[0, 0])
    do = rows_of(qd_ref[0, 1])
    for s in range(SLOTS):
        both = kv_ref[key_slot(pos, s)]
        sc = dot_nt(both[:, :HEAD_DIM], q)
        if s == SLOTS - 1:
            sc = diagonal_cut(sc, pos[1] == b)
        p = jnp.exp2(sc * LOG2_SCALE - (lse + jnp.where(oks[s], 0.0, FAR)))
        ds = p * (dot_nt(both[:, HEAD_DIM:], do) - delta)
        p16[s * BLOCK : (s + 1) * BLOCK, :] = p.astype(jnp.bfloat16)
        ds16[s * BLOCK : (s + 1) * BLOCK, :] = ds.astype(jnp.bfloat16)
    dv[...] += dot_nn(p16[...], do)
    dk[...] += dot_nn(ds16[...], q)
    out_t = dot_nn(vt[...], p16[...])
    dq_t = dot_nn(kt[...], ds16[...]) * SCALE
    for j in range(Q_PER_KV):
        lanes = slice(j * HEAD_DIM, (j + 1) * HEAD_DIM)
        od_ref[0, :, lanes] = out_t[:, lanes].T.astype(jnp.bfloat16)
        od_ref[0, :, ROWS + j * HEAD_DIM : ROWS + (j + 1) * HEAD_DIM] = dq_t[:, lanes].T.astype(jnp.bfloat16)

    @pl.when(b == PLANE - 1)
    def _():
        dkv_ref[...] = jnp.zeros_like(dkv_ref)
        for s in range(SLOTS):
            kz = pos[0] - (SLOTS - 1) + s

            @pl.when(kz >= 0)
            def _():
                at = slice(s * BLOCK, (s + 1) * BLOCK)
                where = jnp.maximum(kz, 0)
                dkv_ref[where, :, :HEAD_DIM] = (dk[at, :] * SCALE).astype(jnp.bfloat16)
                dkv_ref[where, :, HEAD_DIM:] = dv[at, :].astype(jnp.bfloat16)


def body(query, key_proj, value_proj, d_out, block_doc, block_mask):
    pos = jnp.stack([lax.axis_index("z"), lax.axis_index(PLANE_AXES)]).astype(jnp.int32)

    def by_head(m):
        return m.reshape(16, 8, HEAD_DIM).transpose(1, 0, 2)

    mine = jnp.concatenate([by_head(key_proj), by_head(value_proj)], axis=2)
    kv = lax.all_to_all(
        jnp.broadcast_to(mine[None], (ZN, 8, 16, 2 * HEAD_DIM)).reshape(ZN * 8, 16, 2 * HEAD_DIM),
        ("z",) + HEAD_AXES,
        0,
        0,
        tiled=True,
    ).reshape(ZN, BLOCK, 2 * HEAD_DIM)
    qd = lax.all_gather(jnp.stack([query, d_out]), PLANE_AXES)

    smem = pl.BlockSpec(memory_space=pltpu.SMEM)
    qd_spec = pl.BlockSpec((1, 2, BLOCK, ROWS), lambda b: (b, 0, 0, 0))
    kv_spec = pl.BlockSpec((ZN, BLOCK, 2 * HEAD_DIM), lambda b: (0, 0, 0))
    params = pltpu.CompilerParams(vmem_limit_bytes=48 * 2**20, dimension_semantics=("arbitrary",))
    stats = pl.pallas_call(
        stats_kernel,
        grid=(PLANE,),
        in_specs=[smem, smem, smem, qd_spec, kv_spec],
        out_specs=pl.BlockSpec((2, PLANE, ROWS), lambda b: (0, 0, 0)),
        out_shape=jax.ShapeDtypeStruct((2, PLANE, ROWS), jnp.float32),
        compiler_params=params,
        name="stats",
    )(pos, block_doc, block_mask, qd, kv)
    stats = lax.all_gather(stats, PLANE_AXES)
    od, dkv = pl.pallas_call(
        grads_kernel,
        grid=(PLANE,),
        in_specs=[
            smem,
            smem,
            smem,
            pl.BlockSpec((PLANE, 2, PLANE, ROWS), lambda b: (0, 0, 0, 0)),
            qd_spec,
            kv_spec,
        ],
        out_specs=[pl.BlockSpec((1, BLOCK, 2 * ROWS), lambda b: (b, 0, 0)), kv_spec],
        out_shape=[
            jax.ShapeDtypeStruct((PLANE, BLOCK, 2 * ROWS), jnp.bfloat16),
            jax.ShapeDtypeStruct((ZN, BLOCK, 2 * HEAD_DIM), jnp.bfloat16),
        ],
        scratch_shapes=[
            pltpu.VMEM((HEAD_DIM, SLOTS * BLOCK), jnp.bfloat16),
            pltpu.VMEM((HEAD_DIM, SLOTS * BLOCK), jnp.bfloat16),
            pltpu.VMEM((SLOTS * BLOCK, HEAD_DIM), jnp.float32),
            pltpu.VMEM((SLOTS * BLOCK, HEAD_DIM), jnp.float32),
            pltpu.VMEM((SLOTS * BLOCK, ROWS), jnp.bfloat16),
            pltpu.VMEM((SLOTS * BLOCK, ROWS), jnp.bfloat16),
        ],
        compiler_params=params,
        name="grads",
    )(pos, block_doc, block_mask, stats, qd, kv)
    od = lax.psum_scatter(od, PLANE_AXES, scatter_dimension=0)
    back = lax.all_to_all(
        dkv.reshape(ZN * 8, 16, 2 * HEAD_DIM), ("z",) + HEAD_AXES, 0, 0, tiled=True
    )
    summed = jnp.sum(back.reshape(ZN, 8, 16, 2 * HEAD_DIM).astype(jnp.float32), axis=0)
    summed = summed.astype(jnp.bfloat16).transpose(1, 0, 2)
    d_key = summed[:, :, :HEAD_DIM].reshape(16, 8 * HEAD_DIM)
    d_value = summed[:, :, HEAD_DIM:].reshape(16, 8 * HEAD_DIM)
    return od[:, :ROWS], od[:, ROWS:], d_key, d_value


def solution(mesh):
    fine = Mesh(mesh.devices.reshape(8, 4, 2, 2, 4), ("z", "y", "c", "yl", "x"))
    ctx, head = ("z", "y", "c"), ("yl", "x")
    wide, narrow = P(ctx, head), P(ctx + head, None)
    return jax.shard_map(
        body,
        mesh=fine,
        in_specs=(wide, narrow, narrow, wide, P(), P()),
        out_specs=(wide, wide, narrow, narrow),
        check_vma=False,
    )
```

time: 2250 us -> 146 us (0.06); the launches traced: 2210 us -> 146 us
  other arithmetic: 1380 us -> 1.86 us
  local copies, waits for them, and re-layouts: 357 us -> 6.32 us
  waiting for transfers between devices: 386 us -> 46.5 us
  loops' own time: 25.1 us -> 0 us
    select_n x160 -> x0, other arithmetic: 1280 us -> none  [the longest x32 1270 us: allowed_pairs(): jnp.take(block_doc, k_blk)[None, :]]
    gather x230 -> x0, local copies, waits for them, and re-layouts: 304 us -> none  [the longest x128 171 us: allowed_pairs(): jnp.take(block_doc, k_blk)[None, :]]
    ppermute x6 -> x0, waiting for transfers between devices: 224 us -> none  [passed_along(): return lax.ppermute(block, axis, route)]
    all_gather x2 -> x1, waiting for transfers between devices: 155 us -> 12.2 us  [body(): qd = lax.all_gather(jnp.stack([query, d_out]), PLANE_AXES)]
    scatter-add x6 -> x0, other arithmetic: 37.6 us -> none  [body(): buffer = buffer.at[:, landing].add(arrived)]
    reduce_or x32 -> x0, other arithmetic: 29.1 us -> none  [the longest x16 14.6 us: forward_step(): jnp.any(allow)]
    scatter x6 -> x0, local copies, waits for them, and re-layouts: 28.9 us -> none  [body(): buffer = buffer.at[:, movers].set(0.0)]
    another operation x34 -> x0, loops' own time: 25.1 us -> none  [the longest x2 24.5 us: sweep_keys(): return lax.fori_loop(0, turns, one_turn, state)]
  transfers between devices with their start and end apart: 10 -> 3, of which waited for: 9 -> 3; matrix products, arithmetic and copies ran while one was open for 2% -> 2% of each run, Pallas kernels for 0% -> 0%
where the time goes in v1:
time: 146 us
  waiting for transfers between devices  46.5 us (32%)
  blocking collectives  41.8 us (29%)
  Pallas kernels  20.3 us (14%)
  starting transfers between devices  14.9 us (10%)
  between operations  14.1 us (10%)
  local copies, waits for them, and re-layouts  6.32 us (4%)
  other arithmetic  1.86 us (1%)
    all_to_all x1, blocking collectives, body(): lax.all_to_all(dkv.reshape(ZN * 8, 16, 2 * HEAD_DIM), ('z',) + HEAD_AXES,...  27.1 us
    reduce_scatter x1, waiting for transfers between devices, body(): od = lax.psum_scatter(od, PLANE_AXES, scatter_dimension=0)  17.7 us
    all_to_all x1, waiting for transfers between devices, body(): lax.all_to_all(jnp.broadcast_to(mine[None], (ZN, 8, 16, 2 * HEAD_DIM)).re...  16.6 us
    all_to_all x1, starting transfers between devices, body(): lax.all_to_all(jnp.broadcast_to(mine[None], (ZN, 8, 16, 2 * HEAD_DIM)).re...  14.8 us
    all_gather x1, blocking collectives, body(): stats = lax.all_gather(stats, PLANE_AXES)  14.6 us
    pallas_call x1, Pallas kernels, body(): pl.pallas_call(grads_kernel, grid=(PLANE,), in_specs=[smem, smem, smem, p...  12.9 us
    all_gather x1, waiting for transfers between devices, body(): qd = lax.all_gather(jnp.stack([query, d_out]), PLANE_AXES)  12.2 us
    pallas_call x1, Pallas kernels, body(): pl.pallas_call(stats_kernel, grid=(PLANE,), in_specs=[smem, smem, smem, q...  7.41 us
  transfers between devices with their start and end apart: 3, of which 3 were waited for; matrix products, arithmetic and copies ran while one was open for 2% of the time, Pallas kernels for 0%

profile of v1, /device:TPU:6, one launch (start us, length us, event | category | flops | bytes accessed | tf_op | source)
XLA Modules:
  0.0 145.8 jit_solution(8779645360080503581)
XLA Ops:
  7.2 0.0 copy-start.1
  7.2 0.0 copy-start.2
  7.2 0.0 all-gather.4.cloned.1.call-start
  7.2 1.7 %pad_maximum_fusion = bf16[2,128,512]{2,1,0:T(8,128)(2,1)} fusion(bf16[1,128,512]{2,1,0:T(8,128)(2,1)} %bitcast.39, bf16[1,128,512]{2,1,0:T(8,128)(2,1)} %bitcast.40), kind=kLoop, calls=%fused_computation | loop fusion | flops 131072 | bytes 524288 | tf_op jit(solution)/shard_map/stack | solution.py:154
  8.9 0.0 all-gather.4.cloned.1.call-update
  9.0 0.8 copy.17
  9.7 0.8 copy.18
  10.5 0.9 broadcast_in_dim.2
  11.4 14.8 %all-to-all-start = ((bf16[64,16,256]{2,1,0:T(8,128)(2,1)}), bf16[64,16,256]{2,1,0:T(8,128)(2,1)S(1)}, u32[]{:S(2)}, u32[]{:S(2)}) async-start(bf16[64,16,256]{2,1,0:T(8,128)(2,1)} %bitcast.7), calls=%async_computation | async-start | bytes 1048576 | tf_op jit(solution)/shard_map/all_to_all | solution.py:147
  26.2 0.0 reduce-scatter.2.cloned.1.call-start
  26.3 0.1 pad_add_fusion.pos
  26.3 16.6 %all-to-all-done = bf16[64,16,256]{2,1,0:T(8,128)(2,1)S(1)} async-done(((bf16[64,16,256]{2,1,0:T(8,128)(2,1)}), bf16[64,16,256]{2,1,0:T(8,128)(2,1)S(1)}, u32[]{:S(2)}, u32[]{:S(2)}) %all-to-all-start) | async-done | bytes 524320 | tf_op jit(solution)/shard_map/all_to_all | solution.py:147
  42.9 12.2 %all-gather.4.cloned.1.call-done = bf16[16,128,512]{2,1,0:T(8,128)(2,1)} async-done(((bf16[2,128,512]{2,1,0:T(8,128)(2,1)}), bf16[16,128,512]{2,1,0:T(8,128)(2,1)}) %all-gather.4.cloned.1.call-update) | async-done | bytes 2097168 | tf_op jit(solution)/shard_map/all_gather | solution.py:154
  55.1 0.0 copy-done.1
  55.1 0.0 copy-done.2
  55.1 0.0 copy-start
  55.1 1.6 %copy-done = bf16[16,128,512]{2,1,0:T(8,128)(2,1)S(1)} copy-done((bf16[16,128,512]{2,1,0:T(8,128)(2,1)S(1)}, bf16[16,128,512]{2,1,0:T(8,128)(2,1)}, u32[]{:S(2)}) %copy-start) | copy-done | bytes 2097176
  56.7 7.4 %stats.1 = f32[2,8,512]{2,1,0:T(8,128)S(1)} custom-call(s32[2]{0:T(128)S(1)} %pad_add_fusion.pos, s32[64]{0:T(128)S(1)} %copy-done.2, s32[64,64]{1,0:T(8,128)S(1)} %copy-done.1, bf16[8,2,128,512]{3,2,1,0:T(8,128)(2,1)S(1)} %bitcast.28, bf16[8,128,256]{2,1,0:T(8,128)(2,1)S(1)} %bitcast.30), custom_call_target="tpu_custom_call" | custom-call | tf_op jit(solution)/shard_map/stats/pallas_call | solution.py:160
  64.1 14.6 %all-gather.1 = f32[16,8,512]{2,1,0:T(8,128)S(1)} all-gather(f32[2,8,512]{2,1,0:T(8,128)S(1)} %stats.1), channel_id=3, replica_groups=mesh['z'=8,'y'=4,'c'=2,'yl'=2,'x'=4] {'y','c'}, dimensions={0}, use_global_device_ids=true | all-gather | bytes 294912 | tf_op jit(solution)/shard_map/all_gather | solution.py:169
  78.8 12.9 %grads.1 = (bf16[8,128,1024]{2,1,0:T(8,128)(2,1)}, bf16[8,128,256]{2,1,0:T(8,128)(2,1)S(1)}) custom-call(s32[2]{0:T(128)S(1)} %pad_add_fusion.pos, s32[64]{0:T(128)S(1)} %copy-done.2, s32[64,64]{1,0:T(8,128)S(1)} %copy-done.1, f32[8,2,8,512]{3,2,1,0:T(8,128)S(1)} %bitcast.32, bf16[8,2,128,512]{3,2,1,0:T(8,128)(2,1)S(1)} %bitcast.29, ...), custom_call_target="tpu_custom_call" | custom-call | tf_op jit(solution)/shard_map/grads/pallas_call | solution.py:170
  91.7 0.0 reduce-scatter.2.cloned.1.call-update
  91.7 27.1 %all_to_all.10 = bf16[64,16,256]{2,1,0:T(8,128)(2,1)S(1)} all-to-all(bf16[64,16,256]{2,1,0:T(8,128)(2,1)S(1)} %bitcast.33), channel_id=1, replica_groups=mesh['z'=8,'y'=4,'c'=2,'yl'=2,'x'=4] {'z','yl','x'}, dimensions={0} | all-to-all | bytes 1048576 | tf_op jit(solution)/shard_map/all_to_all | solution.py:198
  118.8 0.1 reduce_sum.12
  118.9 0.6 copy_bitcast_fusion
  119.6 17.7 %reduce-scatter.2.cloned.1.call-done = bf16[1,128,1024]{2,1,0:T(8,128)(2,1)} async-done(((bf16[8,128,1024]{2,1,0:T(8,128)(2,1)}), bf16[1,128,1024]{2,1,0:T(8,128)(2,1)}) %reduce-scatter.2.cloned.1.call-update) | async-done | bytes 262160 | tf_op jit(solution)/shard_map/reduce_scatter | solution.py:197
  137.3 1.7 %fusion = (bf16[128,512]{1,0:T(8,128)(2,1)}, bf16[128,512]{1,0:T(8,128)(2,1)}) fusion(bf16[128,1024]{1,0:T(8,128)(2,1)} %bitcast.35), kind=kLoop, calls=%fused_computation.7 | loop fusion | bytes 524288 | tf_op jit(solution)/shard_map/slice | solution.py:205
  (3 shorter events, 0.0 us)
Async XLA Ops:
  7.2 48.0 %copy-start.1 = (s32[64,64]{1,0:T(8,128)S(1)}, s32[64,64]{1,0:T(8,128)}, u32[]{:S(2)}) copy-start(s32[64,64]{1,0:T(8,128)} %mask.3) | copy-start | bytes 49156
  7.2 47.9 %copy-start.2 = (s32[64]{0:T(128)S(1)}, s32[64]{0:T(128)}, u32[]{:S(2)}) copy-start(s32[64]{0:T(128)} %doc.3) | copy-start | bytes 772
  7.2 47.9 %all-gather.4.cloned.1.call-start = ((), (), s32[]{:S(2)}) async-start(), calls=%async_computation.4 | async-start | bytes 2359296 | tf_op jit(solution)/shard_map/all_gather | solution.py:154
  11.4 31.5 %all-to-all-start = ((bf16[64,16,256]{2,1,0:T(8,128)(2,1)}), bf16[64,16,256]{2,1,0:T(8,128)(2,1)S(1)}, u32[]{:S(2)}, u32[]{:S(2)}) async-start(bf16[64,16,256]{2,1,0:T(8,128)(2,1)} %bitcast.7), calls=%async_computation | async-start | bytes 1048576 | tf_op jit(solution)/shard_map/all_to_all | solution.py:147
  26.2 111.1 %reduce-scatter.2.cloned.1.call-start = ((), (), s32[]{:S(2)}) async-start(), calls=%async_computation.3 | async-start | bytes 2359296 | tf_op jit(solution)/shard_map/reduce_scatter | solution.py:197
  55.1 1.6 %copy-start = (bf16[16,128,512]{2,1,0:T(8,128)(2,1)S(1)}, bf16[16,128,512]{2,1,0:T(8,128)(2,1)}, u32[]{:S(2)}) copy-start(bf16[16,128,512]{2,1,0:T(8,128)(2,1)} %all-gather.4.cloned.1.call-done) | copy-start | bytes 6291460
Sparse Core Ops, SparseCore 0:
  10.2 44.9 all-gather.3
  91.8 45.4 reduce-scatter.1

commit v2 on v1

v2 whole, which is shorter than its diff:
```python
import jax
import jax.numpy as jnp
import numpy as np
from jax import lax
from jax.experimental import pallas as pl
from jax.experimental.pallas import tpu as pltpu
from jax.sharding import Mesh
from jax.sharding import PartitionSpec as P

HEAD_DIM = 128
Q_PER_KV = 4
HEADS = 8
BLOCK = 128
PIECE = BLOCK // HEADS
GROUP = 4
YN = 4
ZN = 4
KEYS = ZN * YN
WINDOW = 10
ROWS = Q_PER_KV * BLOCK
NEAR = (WINDOW - 1) * BLOCK
SCALE = HEAD_DIM**-0.5
LOG2_SCALE = SCALE * float(np.log2(np.e))
LOW = -1e30
FAR = 2e30
FAR_BACK = ZN - 1


def dot_nt(a, b):
    return lax.dot_general(a, b, (((1,), (1,)), ((), ())), preferred_element_type=jnp.float32)


def dot_nn(a, b):
    return lax.dot_general(a, b, (((1,), (0,)), ((), ())), preferred_element_type=jnp.float32)


def pack_kernel(q_ref, do_ref, k_ref, v_ref, qd_ref, kv_ref):
    for h in range(HEADS):
        lanes = slice(h * HEAD_DIM, (h + 1) * HEAD_DIM)
        both = jnp.concatenate([k_ref[:, lanes], v_ref[:, lanes]], axis=1)
        for p in range(KEYS):
            kv_ref[h * KEYS + p] = both
    for j in range(Q_PER_KV):
        lanes = slice(j * HEAD_DIM, (j + 1) * HEAD_DIM)
        at = slice(j * BLOCK, (j + 1) * BLOCK)
        qd_ref[0, at, :] = q_ref[:, lanes]
        qd_ref[1, at, :] = do_ref[:, lanes]


def member(pos, j):
    return (pos[1] ^ (j // 2)) * 2 + (pos[3] ^ (j % 2))


def window_of(pos, doc, mask, j):
    zh, zl, y, c = pos[0], pos[1], pos[2], pos[3]
    g = member(pos, j)
    q_blk = 16 * zh + 8 * (g // 2) + 2 * y + g % 2
    ahead = q_blk - (16 * zh + 8 * zl + c)
    last = FAR_BACK * YN + jnp.where(ahead < 0, -1, jnp.minimum(ahead // 2, YN - 1))
    oks = []
    for s in range(WINDOW):
        p = last - (WINDOW - 1) + s
        k_blk = 16 * (zh - FAR_BACK + p // YN) + 8 * zl + 2 * (p % YN) + c
        inside = jnp.maximum(k_blk, 0)
        seen = (inside < q_blk) & (mask[q_blk, inside] == 1) & (doc[q_blk] == doc[inside])
        oks.append((k_blk >= 0) & (seen | (k_blk == q_blk)))
    return pl.multiple_of((last - (WINDOW - 1)) * BLOCK, BLOCK), oks


def owner_of(pos, z):
    return (pos[0] - FAR_BACK + z) & (ZN - 1)


def load_keys(pos, kv_ref, k_scr, v_scr):
    for z in range(ZN):
        owner = owner_of(pos, z)
        for y in range(YN):
            for h in range(HEADS):
                at = (z * YN + y) * BLOCK + h * PIECE
                both = kv_ref[h * KEYS + owner * YN + y]
                k_scr[at : at + PIECE, :] = both[:, :HEAD_DIM]
                v_scr[at : at + PIECE, :] = both[:, HEAD_DIM:]


def diagonal_cut(scores):
    k_at = lax.broadcasted_iota(jnp.int32, (BLOCK, ROWS), 0)
    q_at = lax.broadcasted_iota(jnp.int32, (BLOCK, ROWS), 1) & (BLOCK - 1)
    return jnp.where(k_at <= q_at, scores, LOW)


def stats_kernel(pos, doc, mask, *refs):
    qd_refs, kv_ref = refs[:GROUP], refs[GROUP]
    st_ref, k_scr, v_scr, s_scr, far_scr, row = refs[GROUP + 1 :]
    load_keys(pos, kv_ref, k_scr, v_scr)
    queries = [ref[0] for ref in qd_refs]
    d_outs = [ref[1] for ref in qd_refs]
    windows = [window_of(pos, doc, mask, j) for j in range(GROUP)]
    row[...] = jnp.full((8, ROWS), LOW, jnp.float32)
    for j, (start, oks) in enumerate(windows):

        @pl.when(oks[0])
        def _():
            far = dot_nt(k_scr[pl.ds(start, BLOCK), :], queries[j])
            far_scr[j] = far
            row[j : j + 1, :] = jnp.max(far, axis=0, keepdims=True) * LOG2_SCALE

    tops, totals, inners = [], [], []
    for j, (start, oks) in enumerate(windows):
        near = pl.ds(pl.multiple_of(start + BLOCK, BLOCK), NEAR)
        s_scr[j] = dot_nt(k_scr[near, :], queries[j])
        top = row[j : j + 1, :]
        for s in range(1, WINDOW):
            sc = s_scr[j, (s - 1) * BLOCK : s * BLOCK, :]
            if j == 0 and s == WINDOW - 1:
                sc = diagonal_cut(sc)
                s_scr[j, (s - 1) * BLOCK : s * BLOCK, :] = sc
            most = jnp.max(sc, axis=0, keepdims=True) * LOG2_SCALE
            top = jnp.maximum(top, jnp.where(oks[s], most, LOW))
        dp = dot_nt(v_scr[near, :], d_outs[j])
        total = jnp.zeros((1, ROWS), jnp.float32)
        inner = jnp.zeros((1, ROWS), jnp.float32)
        for s in range(1, WINDOW):
            at = slice((s - 1) * BLOCK, s * BLOCK)
            w = jnp.exp2(s_scr[j, at, :] * LOG2_SCALE - (top + jnp.where(oks[s], 0.0, FAR)))
            total += jnp.sum(w, axis=0, keepdims=True)
            inner += jnp.sum(w * dp[at, :], axis=0, keepdims=True)
        tops.append(top)
        totals.append(total)
        inners.append(inner)
    for j, (start, oks) in enumerate(windows):
        top = tops[j]
        row[0:1, :] = totals[j]
        row[1:2, :] = inners[j]

        @pl.when(oks[0])
        def _():
            w = jnp.exp2(far_scr[j] * LOG2_SCALE - top)
            dp = dot_nt(v_scr[pl.ds(start, BLOCK), :], d_outs[j])
            row[0:1, :] += jnp.sum(w, axis=0, keepdims=True)
            row[1:2, :] += jnp.sum(w * dp, axis=0, keepdims=True)

        total, inner = row[0:1, :], row[1:2, :]
        g = member(pos, j)
        st_ref[pl.ds(g, 1), :] = jnp.where(total > 0.0, top + jnp.log2(jnp.maximum(total, 1.0)), LOW)
        st_ref[pl.ds(GROUP + g, 1), :] = inner / jnp.maximum(total, 1.0)


def row_stats(st_ref, g):
    lse_parts = st_ref[:, pl.ds(g, 1), :]
    delta_parts = st_ref[:, pl.ds(GROUP + g, 1), :]
    most = jnp.max(lse_parts, axis=0)
    lse = most + jnp.log2(jnp.sum(jnp.exp2(lse_parts - most[None]), axis=0))
    delta = jnp.sum(jnp.exp2(lse_parts - lse[None]) * delta_parts, axis=0)
    return lse, delta


def weigh(j, oks, scores, d_probs, lse, delta, p16, ds16):
    for s in range(1, WINDOW):
        at = slice((s - 1) * BLOCK, s * BLOCK)
        sc = scores[at, :]
        if j == 0 and s == WINDOW - 1:
            sc = diagonal_cut(sc)
        p = jnp.exp2(sc * LOG2_SCALE - (lse + jnp.where(oks[s], 0.0, FAR)))
        ds = p * (d_probs[at, :] - delta)
        p16[at, :] = p.astype(jnp.bfloat16)
        ds16[at, :] = ds.astype(jnp.bfloat16)


def weigh_far(scores, d_probs, lse, delta):
    p = jnp.exp2(scores * LOG2_SCALE - lse)
    ds = p * (d_probs - delta)
    return p.astype(jnp.bfloat16), ds.astype(jnp.bfloat16)


def key_grads_kernel(pos, doc, mask, st_ref, *refs):
    qd_refs, kv_ref = refs[:GROUP], refs[GROUP]
    dkv_ref, k_scr, v_scr, dk, dv, p16, ds16 = refs[GROUP + 1 :]
    load_keys(pos, kv_ref, k_scr, v_scr)
    dk[...] = jnp.zeros_like(dk)
    dv[...] = jnp.zeros_like(dv)
    for j in range(GROUP):
        start, oks = window_of(pos, doc, mask, j)
        near = pl.ds(pl.multiple_of(start + BLOCK, BLOCK), NEAR)
        far = pl.ds(start, BLOCK)
        q, do = qd_refs[j][0], qd_refs[j][1]
        lse, delta = row_stats(st_ref, member(pos, j))
        weigh(j, oks, dot_nt(k_scr[near, :], q), dot_nt(v_scr[near, :], do), lse, delta, p16.at[j], ds16.at[j])
        dv[near, :] += dot_nn(p16[j], do)
        dk[near, :] += dot_nn(ds16[j], q)

        @pl.when(oks[0])
        def _():
            p, ds = weigh_far(dot_nt(k_scr[far, :], q), dot_nt(v_scr[far, :], do), lse, delta)
            dv[far, :] += dot_nn(p, do)
            dk[far, :] += dot_nn(ds, q)

    for z in range(ZN):
        owner = owner_of(pos, z)
        for y in range(YN):
            for h in range(HEADS):
                at = (z * YN + y) * BLOCK + h * PIECE
                dkv_ref[h * KEYS + owner * YN + y, :, :HEAD_DIM] = (dk[at : at + PIECE, :] * SCALE).astype(jnp.bfloat16)
                dkv_ref[h * KEYS + owner * YN + y, :, HEAD_DIM:] = dv[at : at + PIECE, :].astype(jnp.bfloat16)


def query_grads_kernel(pos, doc, mask, st_ref, *refs):
    qd_refs, kv_ref = refs[:GROUP], refs[GROUP]
    own_ref, other_ref, k_scr, v_scr, kt, vt, p16, ds16, out_t, dq_t = refs[GROUP + 1 :]
    load_keys(pos, kv_ref, k_scr, v_scr)
    for p in range(KEYS):
        at = slice(p * BLOCK, (p + 1) * BLOCK)
        kt[:, at] = k_scr[at, :].T
        vt[:, at] = v_scr[at, :].T
    for j in range(GROUP):
        start, oks = window_of(pos, doc, mask, j)
        near = pl.ds(pl.multiple_of(start + BLOCK, BLOCK), NEAR)
        far = pl.ds(start, BLOCK)
        q, do = qd_refs[j][0], qd_refs[j][1]
        lse, delta = row_stats(st_ref, member(pos, j))
        weigh(j, oks, dot_nt(k_scr[near, :], q), dot_nt(v_scr[near, :], do), lse, delta, p16.at[j], ds16.at[j])
        out_t[...] = dot_nn(vt[:, near], p16[j])
        dq_t[...] = dot_nn(kt[:, near], ds16[j])

        @pl.when(oks[0])
        def _():
            p, ds = weigh_far(dot_nt(k_scr[far, :], q), dot_nt(v_scr[far, :], do), lse, delta)
            out_t[...] += dot_nn(vt[:, far], p)
            dq_t[...] += dot_nn(kt[:, far], ds)

        to_ref = other_ref if j % 2 else own_ref
        for h in range(Q_PER_KV):
            lanes = slice(h * HEAD_DIM, (h + 1) * HEAD_DIM)
            to_ref[j // 2, :, lanes] = out_t[:, lanes].T.astype(jnp.bfloat16)
            to_ref[j // 2, :, ROWS + h * HEAD_DIM : ROWS + (h + 1) * HEAD_DIM] = (dq_t[:, lanes].T * SCALE).astype(jnp.bfloat16)


def finish_kernel(mine_ref, theirs_ref, back_ref, out_ref, dq_ref, dk_ref, dv_ref):
    total = mine_ref[...].astype(jnp.float32) + theirs_ref[...].astype(jnp.float32)
    out_ref[...] = total[:, :ROWS].astype(jnp.bfloat16)
    dq_ref[...] = total[:, ROWS:].astype(jnp.bfloat16)
    for h in range(HEADS):
        lanes = slice(h * HEAD_DIM, (h + 1) * HEAD_DIM)
        both = sum(back_ref[h * KEYS + p].astype(jnp.float32) for p in range(KEYS))
        dk_ref[:, lanes] = both[:, :HEAD_DIM].astype(jnp.bfloat16)
        dv_ref[:, lanes] = both[:, HEAD_DIM:].astype(jnp.bfloat16)


def bf16(*shape):
    return jax.ShapeDtypeStruct(shape, jnp.bfloat16)


def exchange(block, axis):
    return lax.ppermute(block, axis, [(0, 1), (1, 0)])


def spread(pieces):
    return lax.all_to_all(pieces, ("yl", "x", "zh", "y"), 0, 0, tiled=True)


def call(kernel, operands, smem, out_shape, scratch=(), name=None, limit=40):
    kinds = [pl.BlockSpec(memory_space=pltpu.SMEM if i < smem else pltpu.VMEM) for i in range(len(operands))]
    return pl.pallas_call(
        kernel,
        in_specs=kinds,
        out_shape=out_shape,
        out_specs=jax.tree.map(lambda _: pl.BlockSpec(memory_space=pltpu.VMEM), out_shape),
        scratch_shapes=scratch,
        compiler_params=pltpu.CompilerParams(vmem_limit_bytes=limit * 2**20),
        name=name,
    )(*operands)


def body(query, key_proj, value_proj, d_out, block_doc, block_mask):
    pos = jnp.stack([lax.axis_index(axis) for axis in ("zh", "zl", "y", "c")]).astype(jnp.int32)
    qd, pieces = call(
        pack_kernel,
        (query, d_out, key_proj, value_proj),
        0,
        (bf16(2, ROWS, HEAD_DIM), bf16(HEADS * KEYS, PIECE, 2 * HEAD_DIM)),
        name="pack",
        limit=60,
    )
    kv = spread(pieces)
    above = exchange(qd, "zl")
    held = (qd, exchange(qd, "c"), above, exchange(above, "c"), kv)

    keys_scr = pltpu.VMEM((KEYS * BLOCK, HEAD_DIM), jnp.bfloat16)
    stats = call(
        stats_kernel,
        (pos, block_doc, block_mask, *held),
        3,
        jax.ShapeDtypeStruct((2 * GROUP, ROWS), jnp.float32),
        [
            keys_scr,
            keys_scr,
            pltpu.VMEM((GROUP, NEAR, ROWS), jnp.float32),
            pltpu.VMEM((GROUP, BLOCK, ROWS), jnp.float32),
            pltpu.VMEM((8, ROWS), jnp.float32),
        ],
        name="stats",
    )
    stats = lax.all_gather(stats, ("zl", "c"))
    turned = pltpu.VMEM((HEAD_DIM, KEYS * BLOCK), jnp.bfloat16)
    sums = pltpu.VMEM((KEYS * BLOCK, HEAD_DIM), jnp.float32)
    wide = pltpu.VMEM((GROUP, NEAR, ROWS), jnp.bfloat16)
    flat = pltpu.VMEM((HEAD_DIM, ROWS), jnp.float32)
    operands = (pos, block_doc, block_mask, stats, *held)
    dkv = call(
        key_grads_kernel,
        operands,
        3,
        bf16(HEADS * KEYS, PIECE, 2 * HEAD_DIM),
        [keys_scr, keys_scr, sums, sums, wide, wide],
        name="key_grads",
    )
    back = spread(dkv)
    own, other = call(
        query_grads_kernel,
        operands,
        3,
        (bf16(2, BLOCK, 2 * ROWS), bf16(2, BLOCK, 2 * ROWS)),
        [keys_scr, keys_scr, turned, turned, wide, wide, flat, flat],
        name="query_grads",
    )
    merged = own + exchange(other, "c")
    return call(
        finish_kernel,
        (merged[0], exchange(merged[1], "zl"), back),
        0,
        (bf16(BLOCK, ROWS), bf16(BLOCK, ROWS), bf16(PIECE, HEADS * HEAD_DIM), bf16(PIECE, HEADS * HEAD_DIM)),
        name="finish",
    )


def solution(mesh):
    fine = Mesh(mesh.devices.reshape(4, 2, 4, 2, 2, 4), ("zh", "zl", "y", "c", "yl", "x"))
    ctx, head = ("zh", "zl", "y", "c"), ("yl", "x")
    wide, narrow = P(ctx, head), P(ctx + head, None)
    return jax.shard_map(
        body,
        mesh=fine,
        in_specs=(wide, narrow, narrow, wide, P(), P()),
        out_specs=(wide, wide, narrow, narrow),
        check_vma=False,
    )
```

time: 146 us -> 124 us (0.85)
  blocking collectives: 41.8 us -> 5.25 us
  starting transfers between devices: 14.9 us -> 47.3 us
  between operations: 14.1 us -> 0.76 us
  local copies, waits for them, and re-layouts: 6.32 us -> 0.05 us
  Pallas kernels: 20.3 us -> 23.4 us
  other arithmetic: 1.86 us -> 0.27 us
    ppermute x0 -> x5, waiting for transfers between devices: none -> 44.9 us  [exchange(): return lax.ppermute(block, axis, [(0, 1), (1, 0)])]
    all_to_all x1 -> x0, blocking collectives: 27.1 us -> none  [body(): lax.all_to_all(dkv.reshape(ZN * 8, 16, 2 * HEAD_DIM), ('z',) + HEAD_AXES,...]
    all_to_all x1 -> x2, starting transfers between devices: 14.8 us -> 35.1 us  [spread(): return lax.all_to_all(pieces, ('yl', 'x', 'zh', 'y'), 0, 0, tiled=True)]
    reduce_scatter x1 -> x0, waiting for transfers between devices: 17.7 us -> none  [body(): od = lax.psum_scatter(od, PLANE_AXES, scatter_dimension=0)]
    all_to_all x1 -> x2, waiting for transfers between devices: 16.6 us -> 1.84 us  [spread(): return lax.all_to_all(pieces, ('yl', 'x', 'zh', 'y'), 0, 0, tiled=True)]
    all_gather x1 -> x0, waiting for transfers between devices: 12.2 us -> none  [body(): qd = lax.all_gather(jnp.stack([query, d_out]), PLANE_AXES)]
    ppermute x0 -> x5, starting transfers between devices: none -> 12.1 us  [exchange(): return lax.ppermute(block, axis, [(0, 1), (1, 0)])]
    all_gather x1, blocking collectives: 14.6 us -> 5.25 us  [body(): stats = lax.all_gather(stats, ('zl', 'c'))]
  transfers between devices with their start and end apart: 3 -> 7, of which waited for: 3 -> 5; matrix products, arithmetic and copies ran while one was open for 2% -> 0% of each run, Pallas kernels for 0% -> 5%
where the time goes in v2:
time: 124 us
  starting transfers between devices  47.3 us (38%)
  waiting for transfers between devices  46.8 us (38%)
  Pallas kernels  23.4 us (19%)
  blocking collectives  5.25 us (4%)
    ppermute x5, waiting for transfers between devices, exchange(): return lax.ppermute(block, axis, [(0, 1), (1, 0)])  44.9 us
    all_to_all x2, starting transfers between devices, spread(): return lax.all_to_all(pieces, ('yl', 'x', 'zh', 'y'), 0, 0, tiled=True)  35.1 us
    pallas_call x5, Pallas kernels, call(): pl.pallas_call(kernel, in_specs=kinds, out_shape=out_shape, out_specs=jax...  23.4 us
    ppermute x5, starting transfers between devices, exchange(): return lax.ppermute(block, axis, [(0, 1), (1, 0)])  12.1 us
    all_gather x1, blocking collectives, body(): stats = lax.all_gather(stats, ('zl', 'c'))  5.25 us
  transfers between devices with their start and end apart: 7, of which 5 were waited for; matrix products, arithmetic and copies ran while one was open for 0% of the time, Pallas kernels for 5%

profile of v2, /device:TPU:6, one launch (start us, length us, event | category | flops | bytes accessed | tf_op | source)
XLA Modules:
  0.0 123.7 jit_solution(873093499577096151)
XLA Ops:
  0.6 2.2 %pack.1 = (bf16[2,512,128]{2,1,0:T(8,128)(2,1)}, bf16[128,16,256]{2,1,0:T(8,128)(2,1)}) custom-call(bf16[128,512]{1,0:T(8,128)(2,1)} %q_ref.1, bf16[128,512]{1,0:T(8,128)(2,1)} %do_ref.1, bf16[16,1024]{1,0:T(8,128)(2,1)} %k_ref.1, bf16[16,1024]{1,0:T(8,128)(2,1)} %v_ref.1), custom_call_target="tpu_custom_call" | custom-call | tf_op jit(solution)/shard_map/pack/pallas_call | solution.py:262
  2.8 0.0 copy-start
  2.8 20.2 %all-to-all-start = ((bf16[128,16,256]{2,1,0:T(8,128)(2,1)}), bf16[128,16,256]{2,1,0:T(8,128)(2,1)S(1)}, u32[]{:S(2)}, u32[]{:S(2)}) async-start(bf16[128,16,256]{2,1,0:T(8,128)(2,1)} %get-tuple-element.9), calls=%async_computation | async-start | bytes 2097152 | tf_op jit(solution)/shard_map/all_to_all | solution.py:257
  23.0 0.0 copy-start.1
  23.0 0.0 copy-done
  23.0 3.4 %collective-permute-start.1 = (bf16[2,512,128]{2,1,0:T(8,128)(2,1)S(1)}, bf16[2,512,128]{2,1,0:T(8,128)(2,1)S(1)}, u32[]{:S(2)}, u32[]{:S(2)}) collective-permute-start(bf16[2,512,128]{2,1,0:T(8,128)(2,1)S(1)} %copy-done), channel_id=1, source_target_pairs={{0,64},{64,0},{1,65},{65,1},{2,66},{66,2},{3,67},{67,3},{4,68},{68... | collective-permute-start | bytes 786440 | tf_op jit(solution)/shard_map/ppermute | solution.py:253
  26.4 1.9 %collective-permute-start = (bf16[2,512,128]{2,1,0:T(8,128)(2,1)S(1)}, bf16[2,512,128]{2,1,0:T(8,128)(2,1)S(1)}, u32[]{:S(2)}, u32[]{:S(2)}) collective-permute-start(bf16[2,512,128]{2,1,0:T(8,128)(2,1)S(1)} %copy-done), channel_id=1, source_target_pairs={{0,8},{8,0},{1,9},{9,1},{2,10},{10,2},{3,11},{11,3},{4,12},{12,4},... | collective-permute-start | bytes 786440 | tf_op jit(solution)/shard_map/ppermute | solution.py:253
  28.3 24.1 %collective-permute-done.1.refs_2_ = bf16[2,512,128]{2,1,0:T(8,128)(2,1)S(1)} collective-permute-done((bf16[2,512,128]{2,1,0:T(8,128)(2,1)S(1)}, bf16[2,512,128]{2,1,0:T(8,128)(2,1)S(1)}, u32[]{:S(2)}, u32[]{:S(2)}) %collective-permute-start.1) | collective-permute-done | bytes 262176 | tf_op jit(solution)/shard_map/ppermute | solution.py:253
  52.5 1.9 %collective-permute-start.2 = (bf16[2,512,128]{2,1,0:T(8,128)(2,1)S(1)}, bf16[2,512,128]{2,1,0:T(8,128)(2,1)S(1)}, u32[]{:S(2)}, u32[]{:S(2)}) collective-permute-start(bf16[2,512,128]{2,1,0:T(8,128)(2,1)S(1)} %collective-permute-done.1.refs_2_), channel_id=1, source_target_pairs={{0,8},{8,0},{1,9},{9,1},{2,10},{10,2},{3,11},{11,3},{4,12},{12,4},... | collective-permute-start | bytes 786440 | tf_op jit(solution)/shard_map/ppermute | solution.py:253
  54.4 0.0 copy-start.2
  54.4 0.1 pad_add_fusion.pos
  54.5 0.0 collective-permute-done.refs_1_
  54.5 1.4 %collective-permute-done.2.refs_3_ = bf16[2,512,128]{2,1,0:T(8,128)(2,1)S(1)} collective-permute-done((bf16[2,512,128]{2,1,0:T(8,128)(2,1)S(1)}, bf16[2,512,128]{2,1,0:T(8,128)(2,1)S(1)}, u32[]{:S(2)}, u32[]{:S(2)}) %collective-permute-start.2) | collective-permute-done | bytes 262176 | tf_op jit(solution)/shard_map/ppermute | solution.py:253
  55.9 0.0 all-to-all-done.refs_4_
  55.9 0.0 copy-done.1
  55.9 0.0 copy-done.2
  55.9 5.8 %stats.1 = f32[8,512]{1,0:T(8,128)S(1)} custom-call(s32[4]{0:T(128)S(1)} %pad_add_fusion.pos, s32[64]{0:T(128)S(1)} %copy-done.2, s32[64,64]{1,0:T(8,128)S(1)} %copy-done.1, bf16[2,512,128]{2,1,0:T(8,128)(2,1)S(1)} %copy-done, bf16[2,512,128]{2,1,0:T(8,128)(2,1)S(1)} %collective-permute-done.refs_1_, ...), custom_call_target="tpu_custom_call" | custom-call | tf_op jit(solution)/shard_map/stats/pallas_call | solution.py:262
  61.7 5.2 %all-gather = f32[32,512]{1,0:T(8,128)S(1)} all-gather(f32[8,512]{1,0:T(8,128)S(1)} %stats.1), channel_id=2, replica_groups=mesh['zh'=4,'zl'=2,'y'=4,'c'=2,'yl'=2,'x'=4] {'zl','c'}, dimensions={0}, use_global_device_ids=true | all-gather | bytes 81920 | tf_op jit(solution)/shard_map/all_gather | solution.py:302
  67.0 8.4 %key_grads.1 = bf16[128,16,256]{2,1,0:T(8,128)(2,1)} custom-call(s32[4]{0:T(128)S(1)} %pad_add_fusion.pos, s32[64]{0:T(128)S(1)} %copy-done.2, s32[64,64]{1,0:T(8,128)S(1)} %copy-done.1, f32[4,8,512]{2,1,0:T(8,128)S(1)} %bitcast.9, bf16[2,512,128]{2,1,0:T(8,128)(2,1)S(1)} %copy-done, bf16[2,512,128]{2,1,0:T(8,128)(2,1)S(1)} %collective-permute-done.refs_1_, ...), custom_call_target="tpu_custom_call" | custom-call | tf_op jit(solution)/shard_map/key_grads/pallas_call | solution.py:262
  75.4 14.9 %all-to-all-start.1 = ((bf16[128,16,256]{2,1,0:T(8,128)(2,1)}), bf16[128,16,256]{2,1,0:T(8,128)(2,1)S(1)}, u32[]{:S(2)}, u32[]{:S(2)}) async-start(bf16[128,16,256]{2,1,0:T(8,128)(2,1)} %key_grads.1), calls=%async_computation.1 | async-start | bytes 2097152 | tf_op jit(solution)/shard_map/all_to_all | solution.py:257
  90.3 6.2 %query_grads.1 = (bf16[2,128,1024]{2,1,0:T(8,128)(2,1)S(1)}, bf16[2,128,1024]{2,1,0:T(8,128)(2,1)S(1)}) custom-call(s32[4]{0:T(128)S(1)} %pad_add_fusion.pos, s32[64]{0:T(128)S(1)} %copy-done.2, s32[64,64]{1,0:T(8,128)S(1)} %copy-done.1, f32[4,8,512]{2,1,0:T(8,128)S(1)} %bitcast.10, bf16[2,512,128]{2,1,0:T(8,128)(2,1)S(1)} %copy-done, ...), custom_call_target="tpu_custom_call" | custom-call | tf_op jit(solution)/shard_map/query_grads/pallas_call | solution.py:262
  96.5 1.9 %collective-permute-start.3 = (bf16[2,128,1024]{2,1,0:T(8,128)(2,1)S(1)}, bf16[2,128,1024]{2,1,0:T(8,128)(2,1)S(1)}, u32[]{:S(2)}, u32[]{:S(2)}) collective-permute-start(bf16[2,128,1024]{2,1,0:T(8,128)(2,1)S(1)} %get-tuple-element.11), channel_id=1, source_target_pairs={{0,8},{8,0},{1,9},{9,1},{2,10},{10,2},{3,11},{11,3},{4,12},{12,4},... | collective-permute-start | bytes 1572872 | tf_op jit(solution)/shard_map/ppermute | solution.py:253
  98.4 1.9 %collective-permute-done.3 = bf16[2,128,1024]{2,1,0:T(8,128)(2,1)S(1)} collective-permute-done((bf16[2,128,1024]{2,1,0:T(8,128)(2,1)S(1)}, bf16[2,128,1024]{2,1,0:T(8,128)(2,1)S(1)}, u32[]{:S(2)}, u32[]{:S(2)}) %collective-permute-start.3) | collective-permute-done | bytes 524320 | tf_op jit(solution)/shard_map/ppermute | solution.py:253
  100.3 0.2 add.3
  100.6 3.0 %collective-permute-start.4 = (bf16[128,1024]{1,0:T(8,128)(2,1)S(1)}, bf16[128,1024]{1,0:T(8,128)(2,1)S(1)}, u32[]{:S(2)}, u32[]{:S(2)}) collective-permute-start(bf16[128,1024]{1,0:T(8,128)(2,1)S(1)} %get-tuple-element.12), channel_id=1, source_target_pairs={{0,64},{64,0},{1,65},{65,1},{2,66},{66,2},{3,67},{67,3},{4,68},{68... | collective-permute-start | bytes 786440 | tf_op jit(solution)/shard_map/ppermute | solution.py:253
  103.6 17.5 %collective-permute-done.4.theirs_ref = bf16[128,1024]{1,0:T(8,128)(2,1)S(1)} collective-permute-done((bf16[128,1024]{1,0:T(8,128)(2,1)S(1)}, bf16[128,1024]{1,0:T(8,128)(2,1)S(1)}, u32[]{:S(2)}, u32[]{:S(2)}) %collective-permute-start.4) | collective-permute-done | bytes 262176 | tf_op jit(solution)/shard_map/ppermute | solution.py:253
  121.1 1.8 %all-to-all-done.1.back_ref = bf16[128,16,256]{2,1,0:T(8,128)(2,1)S(1)} async-done(((bf16[128,16,256]{2,1,0:T(8,128)(2,1)}), bf16[128,16,256]{2,1,0:T(8,128)(2,1)S(1)}, u32[]{:S(2)}, u32[]{:S(2)}) %all-to-all-start.1) | async-done | bytes 1048608 | tf_op jit(solution)/shard_map/all_to_all | solution.py:257
  122.9 0.8 finish.1
  (1 shorter events, 0.0 us)
Async XLA Ops:
  2.8 20.2 %copy-start = (bf16[2,512,128]{2,1,0:T(8,128)(2,1)S(1)}, bf16[2,512,128]{2,1,0:T(8,128)(2,1)}, u32[]{:S(2)}) copy-start(bf16[2,512,128]{2,1,0:T(8,128)(2,1)} %get-tuple-element.8.refs_0_) | copy-start | bytes 786436
  2.8 53.1 %all-to-all-start = ((bf16[128,16,256]{2,1,0:T(8,128)(2,1)}), bf16[128,16,256]{2,1,0:T(8,128)(2,1)S(1)}, u32[]{:S(2)}, u32[]{:S(2)}) async-start(bf16[128,16,256]{2,1,0:T(8,128)(2,1)} %get-tuple-element.9), calls=%async_computation | async-start | bytes 2097152 | tf_op jit(solution)/shard_map/all_to_all | solution.py:257
  23.0 32.9 %copy-start.1 = (s32[64,64]{1,0:T(8,128)S(1)}, s32[64,64]{1,0:T(8,128)}, u32[]{:S(2)}) copy-start(s32[64,64]{1,0:T(8,128)} %mask.5) | copy-start | bytes 49156
  23.0 29.5 %collective-permute-start.1 = (bf16[2,512,128]{2,1,0:T(8,128)(2,1)S(1)}, bf16[2,512,128]{2,1,0:T(8,128)(2,1)S(1)}, u32[]{:S(2)}, u32[]{:S(2)}) collective-permute-start(bf16[2,512,128]{2,1,0:T(8,128)(2,1)S(1)} %copy-done), channel_id=1, source_target_pairs={{0,64},{64,0},{1,65},{65,1},{2,66},{66,2},{3,67},{67,3},{4,68},{68... | collective-permute-start | bytes 786440 | tf_op jit(solution)/shard_map/ppermute | solution.py:253
  26.4 28.1 %collective-permute-start = (bf16[2,512,128]{2,1,0:T(8,128)(2,1)S(1)}, bf16[2,512,128]{2,1,0:T(8,128)(2,1)S(1)}, u32[]{:S(2)}, u32[]{:S(2)}) collective-permute-start(bf16[2,512,128]{2,1,0:T(8,128)(2,1)S(1)} %copy-done), channel_id=1, source_target_pairs={{0,8},{8,0},{1,9},{9,1},{2,10},{10,2},{3,11},{11,3},{4,12},{12,4},... | collective-permute-start | bytes 786440 | tf_op jit(solution)/shard_map/ppermute | solution.py:253
  52.5 3.4 %collective-permute-start.2 = (bf16[2,512,128]{2,1,0:T(8,128)(2,1)S(1)}, bf16[2,512,128]{2,1,0:T(8,128)(2,1)S(1)}, u32[]{:S(2)}, u32[]{:S(2)}) collective-permute-start(bf16[2,512,128]{2,1,0:T(8,128)(2,1)S(1)} %collective-permute-done.1.refs_2_), channel_id=1, source_target_pairs={{0,8},{8,0},{1,9},{9,1},{2,10},{10,2},{3,11},{11,3},{4,12},{12,4},... | collective-permute-start | bytes 786440 | tf_op jit(solution)/shard_map/ppermute | solution.py:253
  54.4 1.5 %copy-start.2 = (s32[64]{0:T(128)S(1)}, s32[64]{0:T(128)}, u32[]{:S(2)}) copy-start(s32[64]{0:T(128)} %doc.5) | copy-start | bytes 772
  75.4 47.5 %all-to-all-start.1 = ((bf16[128,16,256]{2,1,0:T(8,128)(2,1)}), bf16[128,16,256]{2,1,0:T(8,128)(2,1)S(1)}, u32[]{:S(2)}, u32[]{:S(2)}) async-start(bf16[128,16,256]{2,1,0:T(8,128)(2,1)} %key_grads.1), calls=%async_computation.1 | async-start | bytes 2097152 | tf_op jit(solution)/shard_map/all_to_all | solution.py:257
  96.5 3.8 %collective-permute-start.3 = (bf16[2,128,1024]{2,1,0:T(8,128)(2,1)S(1)}, bf16[2,128,1024]{2,1,0:T(8,128)(2,1)S(1)}, u32[]{:S(2)}, u32[]{:S(2)}) collective-permute-start(bf16[2,128,1024]{2,1,0:T(8,128)(2,1)S(1)} %get-tuple-element.11), channel_id=1, source_target_pairs={{0,8},{8,0},{1,9},{9,1},{2,10},{10,2},{3,11},{11,3},{4,12},{12,4},... | collective-permute-start | bytes 1572872 | tf_op jit(solution)/shard_map/ppermute | solution.py:253
  100.6 20.5 %collective-permute-start.4 = (bf16[128,1024]{1,0:T(8,128)(2,1)S(1)}, bf16[128,1024]{1,0:T(8,128)(2,1)S(1)}, u32[]{:S(2)}, u32[]{:S(2)}) collective-permute-start(bf16[128,1024]{1,0:T(8,128)(2,1)S(1)} %get-tuple-element.12), channel_id=1, source_target_pairs={{0,64},{64,0},{1,65},{65,1},{2,66},{66,2},{3,67},{67,3},{4,68},{68... | collective-permute-start | bytes 786440 | tf_op jit(solution)/shard_map/ppermute | solution.py:253

commit v3 on v2

--- a/solution.py
+++ b/solution.py
@@ -71,15 +71,15 @@
     return (pos[0] - FAR_BACK + z) & (ZN - 1)
 
 
-def load_keys(pos, kv_ref, k_scr, v_scr):
+def lay_keys(pos, kv_ref, k_ref, v_ref):
     for z in range(ZN):
         owner = owner_of(pos, z)
         for y in range(YN):
             for h in range(HEADS):
                 at = (z * YN + y) * BLOCK + h * PIECE
                 both = kv_ref[h * KEYS + owner * YN + y]
-                k_scr[at : at + PIECE, :] = both[:, :HEAD_DIM]
-                v_scr[at : at + PIECE, :] = both[:, HEAD_DIM:]
+                k_ref[at : at + PIECE, :] = both[:, :HEAD_DIM]
+                v_ref[at : at + PIECE, :] = both[:, HEAD_DIM:]
 
 
 def diagonal_cut(scores):
@@ -88,59 +88,66 @@
     return jnp.where(k_at <= q_at, scores, LOW)
 
 
-def stats_kernel(pos, doc, mask, *refs):
-    qd_refs, kv_ref = refs[:GROUP], refs[GROUP]
-    st_ref, k_scr, v_scr, s_scr, far_scr, row = refs[GROUP + 1 :]
-    load_keys(pos, kv_ref, k_scr, v_scr)
-    queries = [ref[0] for ref in qd_refs]
-    d_outs = [ref[1] for ref in qd_refs]
-    windows = [window_of(pos, doc, mask, j) for j in range(GROUP)]
+def first_stats_kernel(pos, doc, mask, qd_a, qd_b, kv_ref, st_ref, k_ref, v_ref, *scratch):
+    lay_keys(pos, kv_ref, k_ref, v_ref)
+    st_ref[...] = jnp.zeros_like(st_ref)
+    stats_of(pos, doc, mask, (0, 1), (qd_a, qd_b), k_ref, v_ref, st_ref, *scratch)
+
+
+def other_stats_kernel(pos, doc, mask, qd_a, qd_b, k_ref, v_ref, had_ref, st_ref, *scratch):
+    st_ref[...] = had_ref[...]
+    stats_of(pos, doc, mask, (2, 3), (qd_a, qd_b), k_ref, v_ref, st_ref, *scratch)
+
+
+def stats_of(pos, doc, mask, members, qd_refs, k_ref, v_ref, st_ref, s_scr, far_scr, row):
+    windows = [window_of(pos, doc, mask, j) for j in members]
     row[...] = jnp.full((8, ROWS), LOW, jnp.float32)
-    for j, (start, oks) in enumerate(windows):
+    for i, (start, oks) in enumerate(windows):
 
         @pl.when(oks[0])
         def _():
-            far = dot_nt(k_scr[pl.ds(start, BLOCK), :], queries[j])
-            far_scr[j] = far
-            row[j : j + 1, :] = jnp.max(far, axis=0, keepdims=True) * LOG2_SCALE
-
+            far = dot_nt(k_ref[pl.ds(start, BLOCK), :], qd_refs[i][0])
+            far_scr[i] = far
+            row[i : i + 1, :] = jnp.max(far, axis=0, keepdims=True) * LOG2_SCALE
+
+    nears = [pl.ds(pl.multiple_of(start + BLOCK, BLOCK), NEAR) for start, _ in windows]
+    for i, near in enumerate(nears):
+        s_scr[i] = dot_nt(k_ref[near, :], qd_refs[i][0])
+    d_probs = [dot_nt(v_ref[near, :], qd_refs[i][1]) for i, near in enumerate(nears)]
     tops, totals, inners = [], [], []
-    for j, (start, oks) in enumerate(windows):
-        near = pl.ds(pl.multiple_of(start + BLOCK, BLOCK), NEAR)
-        s_scr[j] = dot_nt(k_scr[near, :], queries[j])
-        top = row[j : j + 1, :]
+    for i, (_, oks) in enumerate(windows):
+        top = row[i : i + 1, :]
         for s in range(1, WINDOW):
-            sc = s_scr[j, (s - 1) * BLOCK : s * BLOCK, :]
-            if j == 0 and s == WINDOW - 1:
+            sc = s_scr[i, (s - 1) * BLOCK : s * BLOCK, :]
+            if members[i] == 0 and s == WINDOW - 1:
                 sc = diagonal_cut(sc)
-                s_scr[j, (s - 1) * BLOCK : s * BLOCK, :] = sc
+                s_scr[i, (s - 1) * BLOCK : s * BLOCK, :] = sc
             most = jnp.max(sc, axis=0, keepdims=True) * LOG2_SCALE
             top = jnp.maximum(top, jnp.where(oks[s], most, LOW))
-        dp = dot_nt(v_scr[near, :], d_outs[j])
         total = jnp.zeros((1, ROWS), jnp.float32)
         inner = jnp.zeros((1, ROWS), jnp.float32)
         for s in range(1, WINDOW):
             at = slice((s - 1) * BLOCK, s * BLOCK)
-            w = jnp.exp2(s_scr[j, at, :] * LOG2_SCALE - (top + jnp.where(oks[s], 0.0, FAR)))
+            w = jnp.exp2(s_scr[i, at, :] * LOG2_SCALE - (top + jnp.where(oks[s], 0.0, FAR)))
             total += jnp.sum(w, axis=0, keepdims=True)
-            inner += jnp.sum(w * dp[at, :], axis=0, keepdims=True)
+            inner += jnp.sum(w * d_probs[i][at, :], axis=0, keepdims=True)
         tops.append(top)
         totals.append(total)
         inners.append(inner)
-    for j, (start, oks) in enumerate(windows):
-        top = tops[j]
-        row[0:1, :] = totals[j]
-        row[1:2, :] = inners[j]
+    for i, (start, oks) in enumerate(windows):
+        top = tops[i]
+        row[0:1, :] = totals[i]
+        row[1:2, :] = inners[i]
 
         @pl.when(oks[0])
         def _():
-            w = jnp.exp2(far_scr[j] * LOG2_SCALE - top)
-            dp = dot_nt(v_scr[pl.ds(start, BLOCK), :], d_outs[j])
+            w = jnp.exp2(far_scr[i] * LOG2_SCALE - top)
+            dp = dot_nt(v_ref[pl.ds(start, BLOCK), :], qd_refs[i][1])
             row[0:1, :] += jnp.sum(w, axis=0, keepdims=True)
             row[1:2, :] += jnp.sum(w * dp, axis=0, keepdims=True)
 
         total, inner = row[0:1, :], row[1:2, :]
-        g = member(pos, j)
+        g = member(pos, members[i])
         st_ref[pl.ds(g, 1), :] = jnp.where(total > 0.0, top + jnp.log2(jnp.maximum(total, 1.0)), LOW)
         st_ref[pl.ds(GROUP + g, 1), :] = inner / jnp.maximum(total, 1.0)
 
@@ -173,24 +180,30 @@
 
 
 def key_grads_kernel(pos, doc, mask, st_ref, *refs):
-    qd_refs, kv_ref = refs[:GROUP], refs[GROUP]
-    dkv_ref, k_scr, v_scr, dk, dv, p16, ds16 = refs[GROUP + 1 :]
-    load_keys(pos, kv_ref, k_scr, v_scr)
+    qd_refs = refs[:GROUP]
+    k_ref, v_ref, dkv_ref, dk, dv, p16, ds16 = refs[GROUP:]
     dk[...] = jnp.zeros_like(dk)
     dv[...] = jnp.zeros_like(dv)
+    windows = [window_of(pos, doc, mask, j) for j in range(GROUP)]
+    nears = [pl.ds(pl.multiple_of(start + BLOCK, BLOCK), NEAR) for start, _ in windows]
+    rows = [row_stats(st_ref, member(pos, j)) for j in range(GROUP)]
+
+    def products(j):
+        return dot_nt(k_ref[nears[j], :], qd_refs[j][0]), dot_nt(v_ref[nears[j], :], qd_refs[j][1])
+
+    ready = products(0)
     for j in range(GROUP):
-        start, oks = window_of(pos, doc, mask, j)
-        near = pl.ds(pl.multiple_of(start + BLOCK, BLOCK), NEAR)
+        now, ready = ready, products(j + 1) if j + 1 < GROUP else None
+        weigh(j, windows[j][1], *now, *rows[j], p16.at[j], ds16.at[j])
+        dv[nears[j], :] += dot_nn(p16[j], qd_refs[j][1])
+        dk[nears[j], :] += dot_nn(ds16[j], qd_refs[j][0])
+    for j, (start, oks) in enumerate(windows):
         far = pl.ds(start, BLOCK)
-        q, do = qd_refs[j][0], qd_refs[j][1]
-        lse, delta = row_stats(st_ref, member(pos, j))
-        weigh(j, oks, dot_nt(k_scr[near, :], q), dot_nt(v_scr[near, :], do), lse, delta, p16.at[j], ds16.at[j])
-        dv[near, :] += dot_nn(p16[j], do)
-        dk[near, :] += dot_nn(ds16[j], q)
 
         @pl.when(oks[0])
         def _():
-            p, ds = weigh_far(dot_nt(k_scr[far, :], q), dot_nt(v_scr[far, :], do), lse, delta)
+            q, do = qd_refs[j][0], qd_refs[j][1]
+            p, ds = weigh_far(dot_nt(k_ref[far, :], q), dot_nt(v_ref[far, :], do), *rows[j])
             dv[far, :] += dot_nn(p, do)
             dk[far, :] += dot_nn(ds, q)
 
@@ -204,9 +217,8 @@
 
 
 def query_grads_kernel(pos, doc, mask, st_ref, *refs):
-    qd_refs, kv_ref = refs[:GROUP], refs[GROUP]
-    own_ref, other_ref, k_scr, v_scr, kt, vt, p16, ds16, out_t, dq_t = refs[GROUP + 1 :]
-    load_keys(pos, kv_ref, k_scr, v_scr)
+    qd_refs = refs[:GROUP]
+    k_scr, v_scr, own_ref, other_ref, kt, vt, p16, ds16, out_t, dq_t = refs[GROUP:]
     for p in range(KEYS):
         at = slice(p * BLOCK, (p + 1) * BLOCK)
         kt[:, at] = k_scr[at, :].T
@@ -282,35 +294,32 @@
     )
     kv = spread(pieces)
     above = exchange(qd, "zl")
-    held = (qd, exchange(qd, "c"), above, exchange(above, "c"), kv)
-
-    keys_scr = pltpu.VMEM((KEYS * BLOCK, HEAD_DIM), jnp.bfloat16)
-    stats = call(
-        stats_kernel,
-        (pos, block_doc, block_mask, *held),
-        3,
-        jax.ShapeDtypeStruct((2 * GROUP, ROWS), jnp.float32),
-        [
-            keys_scr,
-            keys_scr,
-            pltpu.VMEM((GROUP, NEAR, ROWS), jnp.float32),
-            pltpu.VMEM((GROUP, BLOCK, ROWS), jnp.float32),
-            pltpu.VMEM((8, ROWS), jnp.float32),
-        ],
-        name="stats",
-    )
+    held = (qd, exchange(qd, "c"), above, exchange(above, "c"))
+
+    keys = bf16(KEYS * BLOCK, HEAD_DIM)
+    rows_out = jax.ShapeDtypeStruct((2 * GROUP, ROWS), jnp.float32)
+    scratch = [
+        pltpu.VMEM((2, NEAR, ROWS), jnp.float32),
+        pltpu.VMEM((2, BLOCK, ROWS), jnp.float32),
+        pltpu.VMEM((8, ROWS), jnp.float32),
+    ]
+    places = (pos, block_doc, block_mask)
+    stats, k_all, v_all = call(
+        first_stats_kernel, (*places, *held[:2], kv), 3, (rows_out, keys, keys), scratch, name="stats_near"
+    )
+    stats = call(other_stats_kernel, (*places, *held[2:], k_all, v_all, stats), 3, rows_out, scratch, name="stats_above")
     stats = lax.all_gather(stats, ("zl", "c"))
     turned = pltpu.VMEM((HEAD_DIM, KEYS * BLOCK), jnp.bfloat16)
     sums = pltpu.VMEM((KEYS * BLOCK, HEAD_DIM), jnp.float32)
     wide = pltpu.VMEM((GROUP, NEAR, ROWS), jnp.bfloat16)
     flat = pltpu.VMEM((HEAD_DIM, ROWS), jnp.float32)
-    operands = (pos, block_doc, block_mask, stats, *held)
+    operands = (*places, stats, *held, k_all, v_all)
     dkv = call(
         key_grads_kernel,
         operands,
         3,
         bf16(HEADS * KEYS, PIECE, 2 * HEAD_DIM),
-        [keys_scr, keys_scr, sums, sums, wide, wide],
+        [sums, sums, wide, wide],
         name="key_grads",
     )
     back = spread(dkv)
@@ -319,7 +328,7 @@
         operands,
         3,
         (bf16(2, BLOCK, 2 * ROWS), bf16(2, BLOCK, 2 * ROWS)),
-        [keys_scr, keys_scr, turned, turned, wide, wide, flat, flat],
+        [turned, turned, wide, wide, flat, flat],
         name="query_grads",
     )
     merged = own + exchange(other, "c")

time: 124 us -> 124 us (level)
    ppermute x5, waiting for transfers between devices: 44.9 us -> 43.5 us  [exchange(): return lax.ppermute(block, axis, [(0, 1), (1, 0)])]
    pallas_call x5 -> x6, Pallas kernels: 23.4 us -> 23.4 us  [call(): pl.pallas_call(kernel, in_specs=kinds, out_shape=out_shape, out_specs=jax...]
  transfers between devices with their start and end apart: 7 -> 7, of which waited for: 5 -> 5; matrix products, arithmetic and copies ran while one was open for 0% -> 0% of each run, Pallas kernels for 5% -> 8%
where the time goes in v3:
time: 124 us; the launch traced here: 123 us
  starting transfers between devices  47.3 us (38%)
  waiting for transfers between devices  45.9 us (37%)
  Pallas kernels  23.4 us (19%)
  blocking collectives  5.43 us (4%)
    ppermute x5, waiting for transfers between devices, exchange(): return lax.ppermute(block, axis, [(0, 1), (1, 0)])  43.5 us
    all_to_all x2, starting transfers between devices, spread(): return lax.all_to_all(pieces, ('yl', 'x', 'zh', 'y'), 0, 0, tiled=True)  35.1 us
    pallas_call x6, Pallas kernels, call(): pl.pallas_call(kernel, in_specs=kinds, out_shape=out_shape, out_specs=jax...  23.4 us
    ppermute x5, starting transfers between devices, exchange(): return lax.ppermute(block, axis, [(0, 1), (1, 0)])  12.1 us
    all_gather x1, blocking collectives, body(): stats = lax.all_gather(stats, ('zl', 'c'))  5.43 us
  transfers between devices with their start and end apart: 7, of which 5 were waited for; matrix products, arithmetic and copies ran while one was open for 0% of the time, Pallas kernels for 8%

profile of v3, /device:TPU:6, one launch (start us, length us, event | category | flops | bytes accessed | tf_op | source)
XLA Modules:
  0.0 123.1 jit_solution(10396710359947487112)
XLA Ops:
  0.6 2.1 %pack.1 = (bf16[2,512,128]{2,1,0:T(8,128)(2,1)}, bf16[128,16,256]{2,1,0:T(8,128)(2,1)}) custom-call(bf16[128,512]{1,0:T(8,128)(2,1)} %q_ref.1, bf16[128,512]{1,0:T(8,128)(2,1)} %do_ref.1, bf16[16,1024]{1,0:T(8,128)(2,1)} %k_ref.1, bf16[16,1024]{1,0:T(8,128)(2,1)} %v_ref.1), custom_call_target="tpu_custom_call" | custom-call | tf_op jit(solution)/shard_map/pack/pallas_call | solution.py:274
  2.8 0.0 copy-start
  2.8 20.2 %all-to-all-start = ((bf16[128,16,256]{2,1,0:T(8,128)(2,1)}), bf16[128,16,256]{2,1,0:T(8,128)(2,1)S(1)}, u32[]{:S(2)}, u32[]{:S(2)}) async-start(bf16[128,16,256]{2,1,0:T(8,128)(2,1)} %get-tuple-element.12), calls=%async_computation | async-start | bytes 2097152 | tf_op jit(solution)/shard_map/all_to_all | solution.py:269
  23.0 0.0 copy-start.1
  23.0 0.0 copy-done
  23.0 3.4 %collective-permute-start = (bf16[2,512,128]{2,1,0:T(8,128)(2,1)S(1)}, bf16[2,512,128]{2,1,0:T(8,128)(2,1)S(1)}, u32[]{:S(2)}, u32[]{:S(2)}) collective-permute-start(bf16[2,512,128]{2,1,0:T(8,128)(2,1)S(1)} %copy-done), channel_id=1, source_target_pairs={{0,64},{64,0},{1,65},{65,1},{2,66},{66,2},{3,67},{67,3},{4,68},{68... | collective-permute-start | bytes 786440 | tf_op jit(solution)/shard_map/ppermute | solution.py:265
  26.4 1.9 %collective-permute-start.2 = (bf16[2,512,128]{2,1,0:T(8,128)(2,1)S(1)}, bf16[2,512,128]{2,1,0:T(8,128)(2,1)S(1)}, u32[]{:S(2)}, u32[]{:S(2)}) collective-permute-start(bf16[2,512,128]{2,1,0:T(8,128)(2,1)S(1)} %copy-done), channel_id=1, source_target_pairs={{0,8},{8,0},{1,9},{9,1},{2,10},{10,2},{3,11},{11,3},{4,12},{12,4},... | collective-permute-start | bytes 786440 | tf_op jit(solution)/shard_map/ppermute | solution.py:265
  28.3 24.1 %collective-permute-done.qd_a.refs_2_ = bf16[2,512,128]{2,1,0:T(8,128)(2,1)S(1)} collective-permute-done((bf16[2,512,128]{2,1,0:T(8,128)(2,1)S(1)}, bf16[2,512,128]{2,1,0:T(8,128)(2,1)S(1)}, u32[]{:S(2)}, u32[]{:S(2)}) %collective-permute-start) | collective-permute-done | bytes 262176 | tf_op jit(solution)/shard_map/ppermute | solution.py:265
  52.5 1.9 %collective-permute-start.1 = (bf16[2,512,128]{2,1,0:T(8,128)(2,1)S(1)}, bf16[2,512,128]{2,1,0:T(8,128)(2,1)S(1)}, u32[]{:S(2)}, u32[]{:S(2)}) collective-permute-start(bf16[2,512,128]{2,1,0:T(8,128)(2,1)S(1)} %collective-permute-done.qd_a.refs_2_), channel_id=1, source_target_pairs={{0,8},{8,0},{1,9},{9,1},{2,10},{10,2},{3,11},{11,3},{4,12},{12,4},... | collective-permute-start | bytes 786440 | tf_op jit(solution)/shard_map/ppermute | solution.py:265
  54.4 0.0 copy-start.2
  54.4 0.1 pad_add_fusion.pos
  54.5 0.0 collective-permute-done.2.qd_b.refs_1_
  54.5 0.6 all-to-all-done.kv_ref
  55.0 0.0 copy-done.1
  55.0 0.0 copy-done.2
  55.0 3.4 %stats_near.1 = (f32[8,512]{1,0:T(8,128)S(1)}, bf16[2048,128]{1,0:T(8,128)(2,1)S(1)}, bf16[2048,128]{1,0:T(8,128)(2,1)S(1)}) custom-call(s32[4]{0:T(128)S(1)} %pad_add_fusion.pos, s32[64]{0:T(128)S(1)} %copy-done.2, s32[64,64]{1,0:T(8,128)S(1)} %copy-done.1, bf16[2,512,128]{2,1,0:T(8,128)(2,1)S(1)} %copy-done, ...), custom_call_target="tpu_custom_call" | custom-call | tf_op jit(solution)/shard_map/stats_near/pallas_call | solution.py:274
  58.4 0.0 collective-permute-done.1.qd_b.refs_3_
  58.4 3.2 %stats_above.1 = f32[8,512]{1,0:T(8,128)S(1)} custom-call(s32[4]{0:T(128)S(1)} %pad_add_fusion.pos, s32[64]{0:T(128)S(1)} %copy-done.2, s32[64,64]{1,0:T(8,128)S(1)} %copy-done.1, bf16[2,512,128]{2,1,0:T(8,128)(2,1)S(1)} %collective-permute-done.qd_a.refs_2_, bf16[2,512,128]{2,1,0:T(8,128)(2,1)S(1)} %collective-permute-done.1.qd_b.refs_3_, ...), custom_call_target="tpu_custom_call" | custom-call | tf_op jit(solution)/shard_map/stats_above/pallas_call | solution.py:274
  61.7 5.4 %all-gather = f32[32,512]{1,0:T(8,128)S(1)} all-gather(f32[8,512]{1,0:T(8,128)S(1)} %stats_above.1), channel_id=2, replica_groups=mesh['zh'=4,'zl'=2,'y'=4,'c'=2,'yl'=2,'x'=4] {'zl','c'}, dimensions={0}, use_global_device_ids=true | all-gather | bytes 81920 | tf_op jit(solution)/shard_map/all_gather | solution.py:311
  67.1 7.6 %key_grads.1 = bf16[128,16,256]{2,1,0:T(8,128)(2,1)} custom-call(s32[4]{0:T(128)S(1)} %pad_add_fusion.pos, s32[64]{0:T(128)S(1)} %copy-done.2, s32[64,64]{1,0:T(8,128)S(1)} %copy-done.1, f32[4,8,512]{2,1,0:T(8,128)S(1)} %bitcast.9, bf16[2,512,128]{2,1,0:T(8,128)(2,1)S(1)} %copy-done, bf16[2,512,128]{2,1,0:T(8,128)(2,1)S(1)} %collective-permute-done.2.qd_b.refs_1_, ...), custom_call_target="tpu_custom_call" | custom-call | tf_op jit(solution)/shard_map/key_grads/pallas_call | solution.py:274
  74.7 14.9 %all-to-all-start.1 = ((bf16[128,16,256]{2,1,0:T(8,128)(2,1)}), bf16[128,16,256]{2,1,0:T(8,128)(2,1)S(1)}, u32[]{:S(2)}, u32[]{:S(2)}) async-start(bf16[128,16,256]{2,1,0:T(8,128)(2,1)} %key_grads.1), calls=%async_computation.1 | async-start | bytes 2097152 | tf_op jit(solution)/shard_map/all_to_all | solution.py:269
  89.7 6.1 %query_grads.1 = (bf16[2,128,1024]{2,1,0:T(8,128)(2,1)S(1)}, bf16[2,128,1024]{2,1,0:T(8,128)(2,1)S(1)}) custom-call(s32[4]{0:T(128)S(1)} %pad_add_fusion.pos, s32[64]{0:T(128)S(1)} %copy-done.2, s32[64,64]{1,0:T(8,128)S(1)} %copy-done.1, f32[4,8,512]{2,1,0:T(8,128)S(1)} %bitcast.10, bf16[2,512,128]{2,1,0:T(8,128)(2,1)S(1)} %copy-done, ...), custom_call_target="tpu_custom_call" | custom-call | tf_op jit(solution)/shard_map/query_grads/pallas_call | solution.py:274
  95.8 1.9 %collective-permute-start.3 = (bf16[2,128,1024]{2,1,0:T(8,128)(2,1)S(1)}, bf16[2,128,1024]{2,1,0:T(8,128)(2,1)S(1)}, u32[]{:S(2)}, u32[]{:S(2)}) collective-permute-start(bf16[2,128,1024]{2,1,0:T(8,128)(2,1)S(1)} %get-tuple-element.17), channel_id=1, source_target_pairs={{0,8},{8,0},{1,9},{9,1},{2,10},{10,2},{3,11},{11,3},{4,12},{12,4},... | collective-permute-start | bytes 1572872 | tf_op jit(solution)/shard_map/ppermute | solution.py:265
  97.8 1.9 %collective-permute-done.3 = bf16[2,128,1024]{2,1,0:T(8,128)(2,1)S(1)} collective-permute-done((bf16[2,128,1024]{2,1,0:T(8,128)(2,1)S(1)}, bf16[2,128,1024]{2,1,0:T(8,128)(2,1)S(1)}, u32[]{:S(2)}, u32[]{:S(2)}) %collective-permute-start.3) | collective-permute-done | bytes 524320 | tf_op jit(solution)/shard_map/ppermute | solution.py:265
  99.6 0.2 add.3
  99.9 3.0 %collective-permute-start.4 = (bf16[128,1024]{1,0:T(8,128)(2,1)S(1)}, bf16[128,1024]{1,0:T(8,128)(2,1)S(1)}, u32[]{:S(2)}, u32[]{:S(2)}) collective-permute-start(bf16[128,1024]{1,0:T(8,128)(2,1)S(1)} %get-tuple-element.18), channel_id=1, source_target_pairs={{0,64},{64,0},{1,65},{65,1},{2,66},{66,2},{3,67},{67,3},{4,68},{68... | collective-permute-start | bytes 786440 | tf_op jit(solution)/shard_map/ppermute | solution.py:265
  102.9 17.5 %collective-permute-done.4.theirs_ref = bf16[128,1024]{1,0:T(8,128)(2,1)S(1)} collective-permute-done((bf16[128,1024]{1,0:T(8,128)(2,1)S(1)}, bf16[128,1024]{1,0:T(8,128)(2,1)S(1)}, u32[]{:S(2)}, u32[]{:S(2)}) %collective-permute-start.4) | collective-permute-done | bytes 262176 | tf_op jit(solution)/shard_map/ppermute | solution.py:265
  120.4 1.9 %all-to-all-done.1.back_ref = bf16[128,16,256]{2,1,0:T(8,128)(2,1)S(1)} async-done(((bf16[128,16,256]{2,1,0:T(8,128)(2,1)}), bf16[128,16,256]{2,1,0:T(8,128)(2,1)S(1)}, u32[]{:S(2)}, u32[]{:S(2)}) %all-to-all-start.1) | async-done | bytes 1048608 | tf_op jit(solution)/shard_map/all_to_all | solution.py:269
  122.2 0.8 finish.1
  (1 shorter events, 0.0 us)
Async XLA Ops:
  2.8 20.2 %copy-start = (bf16[2,512,128]{2,1,0:T(8,128)(2,1)S(1)}, bf16[2,512,128]{2,1,0:T(8,128)(2,1)}, u32[]{:S(2)}) copy-start(bf16[2,512,128]{2,1,0:T(8,128)(2,1)} %get-tuple-element.11.qd_a.refs_0_) | copy-start | bytes 786436
  2.8 52.3 %all-to-all-start = ((bf16[128,16,256]{2,1,0:T(8,128)(2,1)}), bf16[128,16,256]{2,1,0:T(8,128)(2,1)S(1)}, u32[]{:S(2)}, u32[]{:S(2)}) async-start(bf16[128,16,256]{2,1,0:T(8,128)(2,1)} %get-tuple-element.12), calls=%async_computation | async-start | bytes 2097152 | tf_op jit(solution)/shard_map/all_to_all | solution.py:269
  23.0 32.1 %copy-start.1 = (s32[64,64]{1,0:T(8,128)S(1)}, s32[64,64]{1,0:T(8,128)}, u32[]{:S(2)}) copy-start(s32[64,64]{1,0:T(8,128)} %mask.7) | copy-start | bytes 49156
  23.0 29.5 %collective-permute-start = (bf16[2,512,128]{2,1,0:T(8,128)(2,1)S(1)}, bf16[2,512,128]{2,1,0:T(8,128)(2,1)S(1)}, u32[]{:S(2)}, u32[]{:S(2)}) collective-permute-start(bf16[2,512,128]{2,1,0:T(8,128)(2,1)S(1)} %copy-done), channel_id=1, source_target_pairs={{0,64},{64,0},{1,65},{65,1},{2,66},{66,2},{3,67},{67,3},{4,68},{68... | collective-permute-start | bytes 786440 | tf_op jit(solution)/shard_map/ppermute | solution.py:265
  26.4 28.1 %collective-permute-start.2 = (bf16[2,512,128]{2,1,0:T(8,128)(2,1)S(1)}, bf16[2,512,128]{2,1,0:T(8,128)(2,1)S(1)}, u32[]{:S(2)}, u32[]{:S(2)}) collective-permute-start(bf16[2,512,128]{2,1,0:T(8,128)(2,1)S(1)} %copy-done), channel_id=1, source_target_pairs={{0,8},{8,0},{1,9},{9,1},{2,10},{10,2},{3,11},{11,3},{4,12},{12,4},... | collective-permute-start | bytes 786440 | tf_op jit(solution)/shard_map/ppermute | solution.py:265
  52.5 6.0 %collective-permute-start.1 = (bf16[2,512,128]{2,1,0:T(8,128)(2,1)S(1)}, bf16[2,512,128]{2,1,0:T(8,128)(2,1)S(1)}, u32[]{:S(2)}, u32[]{:S(2)}) collective-permute-start(bf16[2,512,128]{2,1,0:T(8,128)(2,1)S(1)} %collective-permute-done.qd_a.refs_2_), channel_id=1, source_target_pairs={{0,8},{8,0},{1,9},{9,1},{2,10},{10,2},{3,11},{11,3},{4,12},{12,4},... | collective-permute-start | bytes 786440 | tf_op jit(solution)/shard_map/ppermute | solution.py:265
  54.4 0.7 copy-start.2
  74.7 47.5 %all-to-all-start.1 = ((bf16[128,16,256]{2,1,0:T(8,128)(2,1)}), bf16[128,16,256]{2,1,0:T(8,128)(2,1)S(1)}, u32[]{:S(2)}, u32[]{:S(2)}) async-start(bf16[128,16,256]{2,1,0:T(8,128)(2,1)} %key_grads.1), calls=%async_computation.1 | async-start | bytes 2097152 | tf_op jit(solution)/shard_map/all_to_all | solution.py:269
  95.8 3.8 %collective-permute-start.3 = (bf16[2,128,1024]{2,1,0:T(8,128)(2,1)S(1)}, bf16[2,128,1024]{2,1,0:T(8,128)(2,1)S(1)}, u32[]{:S(2)}, u32[]{:S(2)}) collective-permute-start(bf16[2,128,1024]{2,1,0:T(8,128)(2,1)S(1)} %get-tuple-element.17), channel_id=1, source_target_pairs={{0,8},{8,0},{1,9},{9,1},{2,10},{10,2},{3,11},{11,3},{4,12},{12,4},... | collective-permute-start | bytes 1572872 | tf_op jit(solution)/shard_map/ppermute | solution.py:265
  99.9 20.5 %collective-permute-start.4 = (bf16[128,1024]{1,0:T(8,128)(2,1)S(1)}, bf16[128,1024]{1,0:T(8,128)(2,1)S(1)}, u32[]{:S(2)}, u32[]{:S(2)}) collective-permute-start(bf16[128,1024]{1,0:T(8,128)(2,1)S(1)} %get-tuple-element.18), channel_id=1, source_target_pairs={{0,64},{64,0},{1,65},{65,1},{2,66},{66,2},{3,67},{67,3},{4,68},{68... | collective-permute-start | bytes 786440 | tf_op jit(solution)/shard_map/ppermute | solution.py:265

commit v4 on v3

--- a/solution.py
+++ b/solution.py
@@ -34,12 +34,15 @@
     return lax.dot_general(a, b, (((1,), (0,)), ((), ())), preferred_element_type=jnp.float32)
 
 
-def pack_kernel(q_ref, do_ref, k_ref, v_ref, qd_ref, kv_ref):
+def pack_keys_kernel(k_ref, v_ref, kv_ref):
     for h in range(HEADS):
         lanes = slice(h * HEAD_DIM, (h + 1) * HEAD_DIM)
         both = jnp.concatenate([k_ref[:, lanes], v_ref[:, lanes]], axis=1)
         for p in range(KEYS):
             kv_ref[h * KEYS + p] = both
+
+
+def pack_queries_kernel(q_ref, do_ref, qd_ref):
     for j in range(Q_PER_KV):
         lanes = slice(j * HEAD_DIM, (j + 1) * HEAD_DIM)
         at = slice(j * BLOCK, (j + 1) * BLOCK)
@@ -284,17 +287,18 @@
 
 def body(query, key_proj, value_proj, d_out, block_doc, block_mask):
     pos = jnp.stack([lax.axis_index(axis) for axis in ("zh", "zl", "y", "c")]).astype(jnp.int32)
-    qd, pieces = call(
-        pack_kernel,
-        (query, d_out, key_proj, value_proj),
+    pieces = call(
+        pack_keys_kernel,
+        (key_proj, value_proj),
         0,
-        (bf16(2, ROWS, HEAD_DIM), bf16(HEADS * KEYS, PIECE, 2 * HEAD_DIM)),
-        name="pack",
+        bf16(HEADS * KEYS, PIECE, 2 * HEAD_DIM),
+        name="pack_keys",
         limit=60,
     )
+    qd = call(pack_queries_kernel, (query, d_out), 0, bf16(2, ROWS, HEAD_DIM), name="pack_queries")
     kv = spread(pieces)
     above = exchange(qd, "zl")
-    held = (qd, exchange(qd, "c"), above, exchange(above, "c"))
+    held = (qd, exchange(qd, "c"))
 
     keys = bf16(KEYS * BLOCK, HEAD_DIM)
     rows_out = jax.ShapeDtypeStruct((2 * GROUP, ROWS), jnp.float32)
@@ -307,6 +311,8 @@
     stats, k_all, v_all = call(
         first_stats_kernel, (*places, *held[:2], kv), 3, (rows_out, keys, keys), scratch, name="stats_near"
     )
+    above, stats, k_all, v_all = lax.optimization_barrier((above, stats, k_all, v_all))
+    held += (above, exchange(above, "c"))
     stats = call(other_stats_kernel, (*places, *held[2:], k_all, v_all, stats), 3, rows_out, scratch, name="stats_above")
     stats = lax.all_gather(stats, ("zl", "c"))
     turned = pltpu.VMEM((HEAD_DIM, KEYS * BLOCK), jnp.bfloat16)

time: 124 us -> 121 us (0.976)
  starting transfers between devices: 47.3 us -> 41.3 us
  waiting for transfers between devices: 45.9 us -> 49.3 us
    all_to_all x2, waiting for transfers between devices: 2.42 us -> 28.4 us  [spread(): return lax.all_to_all(pieces, ('yl', 'x', 'zh', 'y'), 0, 0, tiled=True)]
    ppermute x5, waiting for transfers between devices: 43.5 us -> 20.9 us  [exchange(): return lax.ppermute(block, axis, [(0, 1), (1, 0)])]
    all_to_all x2, starting transfers between devices: 35.1 us -> 29.2 us  [spread(): return lax.all_to_all(pieces, ('yl', 'x', 'zh', 'y'), 0, 0, tiled=True)]
    pallas_call x6 -> x7, Pallas kernels: 23.4 us -> 23.1 us  [call(): pl.pallas_call(kernel, in_specs=kinds, out_shape=out_shape, out_specs=jax...]
where the time goes in v4:
time: 121 us; the launch traced here: 120 us
  waiting for transfers between devices  49.3 us (41%)
  starting transfers between devices  41.3 us (34%)
  Pallas kernels  23.1 us (19%)
  blocking collectives  5.43 us (4%)
    all_to_all x2, starting transfers between devices, spread(): return lax.all_to_all(pieces, ('yl', 'x', 'zh', 'y'), 0, 0, tiled=True)  29.2 us
    all_to_all x2, waiting for transfers between devices, spread(): return lax.all_to_all(pieces, ('yl', 'x', 'zh', 'y'), 0, 0, tiled=True)  28.4 us
    pallas_call x7, Pallas kernels, call(): pl.pallas_call(kernel, in_specs=kinds, out_shape=out_shape, out_specs=jax...  23.1 us
    ppermute x5, waiting for transfers between devices, exchange(): return lax.ppermute(block, axis, [(0, 1), (1, 0)])  20.9 us
    ppermute x5, starting transfers between devices, exchange(): return lax.ppermute(block, axis, [(0, 1), (1, 0)])  12.1 us
    all_gather x1, blocking collectives, body(): stats = lax.all_gather(stats, ('zl', 'c'))  5.43 us
  transfers between devices with their start and end apart: 7, of which 5 were waited for; matrix products, arithmetic and copies ran while one was open for 0% of the time, Pallas kernels for 8%

profile of v4, /device:TPU:6, one launch (start us, length us, event | category | flops | bytes accessed | tf_op | source)
XLA Modules:
  0.0 120.2 jit_solution(4730744273708451249)
XLA Ops:
  0.6 1.8 %pack_keys.1 = bf16[128,16,256]{2,1,0:T(8,128)(2,1)} custom-call(bf16[16,1024]{1,0:T(8,128)(2,1)} %k_ref.1, bf16[16,1024]{1,0:T(8,128)(2,1)} %v_ref.1), custom_call_target="tpu_custom_call" | custom-call | tf_op jit(solution)/shard_map/pack_keys/pallas_call | solution.py:277
  2.5 0.0 copy-start.1
  2.5 0.0 copy-start.2
  2.5 20.2 %all-to-all-start = ((bf16[128,16,256]{2,1,0:T(8,128)(2,1)}), bf16[128,16,256]{2,1,0:T(8,128)(2,1)S(1)}, u32[]{:S(2)}, u32[]{:S(2)}) async-start(bf16[128,16,256]{2,1,0:T(8,128)(2,1)} %pack_keys.1), calls=%async_computation | async-start | bytes 2097152 | tf_op jit(solution)/shard_map/all_to_all | solution.py:272
  22.6 0.0 copy-done.1
  22.7 0.0 copy-done.2
  22.7 0.0 copy-start
  22.7 1.9 %collective-permute-start.1 = (bf16[2,512,128]{2,1,0:T(8,128)(2,1)S(1)}, bf16[2,512,128]{2,1,0:T(8,128)(2,1)S(1)}, u32[]{:S(2)}, u32[]{:S(2)}) collective-permute-start(bf16[2,512,128]{2,1,0:T(8,128)(2,1)S(1)} %pack_queries.1.qd_a.refs_0_), channel_id=1, source_target_pairs={{0,8},{8,0},{1,9},{9,1},{2,10},{10,2},{3,11},{11,3},{4,12},{12,4},... | collective-permute-start | bytes 786440 | tf_op jit(solution)/shard_map/ppermute | solution.py:268
  24.7 3.4 %collective-permute-start = (bf16[2,512,128]{2,1,0:T(8,128)(2,1)S(1)}, bf16[2,512,128]{2,1,0:T(8,128)(2,1)S(1)}, u32[]{:S(2)}, u32[]{:S(2)}) collective-permute-start(bf16[2,512,128]{2,1,0:T(8,128)(2,1)S(1)} %pack_queries.1.qd_a.refs_0_), channel_id=1, source_target_pairs={{0,64},{64,0},{1,65},{65,1},{2,66},{66,2},{3,67},{67,3},{4,68},{68... | collective-permute-start | bytes 786440 | tf_op jit(solution)/shard_map/ppermute | solution.py:268
  28.1 0.0 copy-start.3
  28.1 0.1 pad_add_fusion.pos
  28.2 0.0 collective-permute-done.1.qd_b.refs_1_
  28.2 26.6 %all-to-all-done.kv_ref = bf16[128,16,256]{2,1,0:T(8,128)(2,1)S(1)} async-done(((bf16[128,16,256]{2,1,0:T(8,128)(2,1)}), bf16[128,16,256]{2,1,0:T(8,128)(2,1)S(1)}, u32[]{:S(2)}, u32[]{:S(2)}) %all-to-all-start) | async-done | bytes 1048608 | tf_op jit(solution)/shard_map/all_to_all | solution.py:272
  54.7 0.0 copy-done
  54.7 0.0 copy-done.3
  54.7 3.4 %stats_near.1 = (f32[8,512]{1,0:T(8,128)S(1)}, bf16[2048,128]{1,0:T(8,128)(2,1)S(1)}, bf16[2048,128]{1,0:T(8,128)(2,1)S(1)}) custom-call(s32[4]{0:T(128)S(1)} %pad_add_fusion.pos, s32[64]{0:T(128)S(1)} %copy-done.3, s32[64,64]{1,0:T(8,128)S(1)} %copy-done, bf16[2,512,128]{2,1,0:T(8,128)(2,1)S(1)} %pack_queries.1.qd_a.refs_0_, ...), custom_call_target="tpu_custom_call" | custom-call | tf_op jit(solution)/shard_map/stats_near/pallas_call | solution.py:277
  58.1 0.0 collective-permute-done.qd_a.refs_2_
  58.1 1.9 %collective-permute-start.2 = (bf16[2,512,128]{2,1,0:T(8,128)(2,1)S(1)}, bf16[2,512,128]{2,1,0:T(8,128)(2,1)S(1)}, u32[]{:S(2)}, u32[]{:S(2)}) collective-permute-start(bf16[2,512,128]{2,1,0:T(8,128)(2,1)S(1)} %collective-permute-done.qd_a.refs_2_), channel_id=1, source_target_pairs={{0,8},{8,0},{1,9},{9,1},{2,10},{10,2},{3,11},{11,3},{4,12},{12,4},... | collective-permute-start | bytes 786440 | tf_op jit(solution)/shard_map/ppermute | solution.py:268
  60.0 1.5 %collective-permute-done.2.qd_b.refs_3_ = bf16[2,512,128]{2,1,0:T(8,128)(2,1)S(1)} collective-permute-done((bf16[2,512,128]{2,1,0:T(8,128)(2,1)S(1)}, bf16[2,512,128]{2,1,0:T(8,128)(2,1)S(1)}, u32[]{:S(2)}, u32[]{:S(2)}) %collective-permute-start.2) | collective-permute-done | bytes 262176 | tf_op jit(solution)/shard_map/ppermute | solution.py:268
  61.5 3.2 %stats_above.1 = f32[8,512]{1,0:T(8,128)S(1)} custom-call(s32[4]{0:T(128)S(1)} %pad_add_fusion.pos, s32[64]{0:T(128)S(1)} %copy-done.3, s32[64,64]{1,0:T(8,128)S(1)} %copy-done, bf16[2,512,128]{2,1,0:T(8,128)(2,1)S(1)} %collective-permute-done.qd_a.refs_2_, bf16[2,512,128]{2,1,0:T(8,128)(2,1)S(1)} %collective-permute-done.2.qd_b.refs_3_, ...), custom_call_target="tpu_custom_call" | custom-call | tf_op jit(solution)/shard_map/stats_above/pallas_call | solution.py:277
  64.8 5.4 %all-gather = f32[32,512]{1,0:T(8,128)S(1)} all-gather(f32[8,512]{1,0:T(8,128)S(1)} %stats_above.1), channel_id=2, replica_groups=mesh['zh'=4,'zl'=2,'y'=4,'c'=2,'yl'=2,'x'=4] {'zl','c'}, dimensions={0}, use_global_device_ids=true | all-gather | bytes 81920 | tf_op jit(solution)/shard_map/all_gather | solution.py:317
  70.2 7.6 %key_grads.1 = bf16[128,16,256]{2,1,0:T(8,128)(2,1)} custom-call(s32[4]{0:T(128)S(1)} %pad_add_fusion.pos, s32[64]{0:T(128)S(1)} %copy-done.3, s32[64,64]{1,0:T(8,128)S(1)} %copy-done, f32[4,8,512]{2,1,0:T(8,128)S(1)} %bitcast.9, bf16[2,512,128]{2,1,0:T(8,128)(2,1)S(1)} %pack_queries.1.qd_a.refs_0_, ...), custom_call_target="tpu_custom_call" | custom-call | tf_op jit(solution)/shard_map/key_grads/pallas_call | solution.py:277
  77.8 9.0 %all-to-all-start.1 = ((bf16[128,16,256]{2,1,0:T(8,128)(2,1)}), bf16[128,16,256]{2,1,0:T(8,128)(2,1)S(1)}, u32[]{:S(2)}, u32[]{:S(2)}) async-start(bf16[128,16,256]{2,1,0:T(8,128)(2,1)} %key_grads.1), calls=%async_computation.1 | async-start | bytes 2097152 | tf_op jit(solution)/shard_map/all_to_all | solution.py:272
  86.8 6.1 %query_grads.1 = (bf16[2,128,1024]{2,1,0:T(8,128)(2,1)S(1)}, bf16[2,128,1024]{2,1,0:T(8,128)(2,1)S(1)}) custom-call(s32[4]{0:T(128)S(1)} %pad_add_fusion.pos, s32[64]{0:T(128)S(1)} %copy-done.3, s32[64,64]{1,0:T(8,128)S(1)} %copy-done, f32[4,8,512]{2,1,0:T(8,128)S(1)} %bitcast.10, bf16[2,512,128]{2,1,0:T(8,128)(2,1)S(1)} %pack_queries.1.qd_a.refs_0_, ...), custom_call_target="tpu_custom_call" | custom-call | tf_op jit(solution)/shard_map/query_grads/pallas_call | solution.py:277
  93.0 1.9 %collective-permute-start.3 = (bf16[2,128,1024]{2,1,0:T(8,128)(2,1)S(1)}, bf16[2,128,1024]{2,1,0:T(8,128)(2,1)S(1)}, u32[]{:S(2)}, u32[]{:S(2)}) collective-permute-start(bf16[2,128,1024]{2,1,0:T(8,128)(2,1)S(1)} %get-tuple-element.21), channel_id=1, source_target_pairs={{0,8},{8,0},{1,9},{9,1},{2,10},{10,2},{3,11},{11,3},{4,12},{12,4},... | collective-permute-start | bytes 1572872 | tf_op jit(solution)/shard_map/ppermute | solution.py:268
  94.9 1.9 %collective-permute-done.3 = bf16[2,128,1024]{2,1,0:T(8,128)(2,1)S(1)} collective-permute-done((bf16[2,128,1024]{2,1,0:T(8,128)(2,1)S(1)}, bf16[2,128,1024]{2,1,0:T(8,128)(2,1)S(1)}, u32[]{:S(2)}, u32[]{:S(2)}) %collective-permute-start.3) | collective-permute-done | bytes 524320 | tf_op jit(solution)/shard_map/ppermute | solution.py:268
  96.8 0.2 add.3
  97.0 3.0 %collective-permute-start.4 = (bf16[128,1024]{1,0:T(8,128)(2,1)S(1)}, bf16[128,1024]{1,0:T(8,128)(2,1)S(1)}, u32[]{:S(2)}, u32[]{:S(2)}) collective-permute-start(bf16[128,1024]{1,0:T(8,128)(2,1)S(1)} %get-tuple-element.22), channel_id=1, source_target_pairs={{0,64},{64,0},{1,65},{65,1},{2,66},{66,2},{3,67},{67,3},{4,68},{68... | collective-permute-start | bytes 786440 | tf_op jit(solution)/shard_map/ppermute | solution.py:268
  100.0 17.5 %collective-permute-done.4.theirs_ref = bf16[128,1024]{1,0:T(8,128)(2,1)S(1)} collective-permute-done((bf16[128,1024]{1,0:T(8,128)(2,1)S(1)}, bf16[128,1024]{1,0:T(8,128)(2,1)S(1)}, u32[]{:S(2)}, u32[]{:S(2)}) %collective-permute-start.4) | collective-permute-done | bytes 262176 | tf_op jit(solution)/shard_map/ppermute | solution.py:268
  117.6 1.8 %all-to-all-done.1.back_ref = bf16[128,16,256]{2,1,0:T(8,128)(2,1)S(1)} async-done(((bf16[128,16,256]{2,1,0:T(8,128)(2,1)}), bf16[128,16,256]{2,1,0:T(8,128)(2,1)S(1)}, u32[]{:S(2)}, u32[]{:S(2)}) %all-to-all-start.1) | async-done | bytes 1048608 | tf_op jit(solution)/shard_map/all_to_all | solution.py:272
  119.4 0.8 finish.1
  (2 shorter events, 0.1 us)
Async XLA Ops:
  2.5 20.2 %copy-start.1 = (bf16[128,512]{1,0:T(8,128)(2,1)S(1)}, bf16[128,512]{1,0:T(8,128)(2,1)}, u32[]{:S(2)}) copy-start(bf16[128,512]{1,0:T(8,128)(2,1)} %q_ref.1) | copy-start | bytes 393220
  2.5 20.2 %copy-start.2 = (bf16[128,512]{1,0:T(8,128)(2,1)S(1)}, bf16[128,512]{1,0:T(8,128)(2,1)}, u32[]{:S(2)}) copy-start(bf16[128,512]{1,0:T(8,128)(2,1)} %do_ref.1) | copy-start | bytes 393220
  2.5 52.3 %all-to-all-start = ((bf16[128,16,256]{2,1,0:T(8,128)(2,1)}), bf16[128,16,256]{2,1,0:T(8,128)(2,1)S(1)}, u32[]{:S(2)}, u32[]{:S(2)}) async-start(bf16[128,16,256]{2,1,0:T(8,128)(2,1)} %pack_keys.1), calls=%async_computation | async-start | bytes 2097152 | tf_op jit(solution)/shard_map/all_to_all | solution.py:272
  22.7 32.0 %copy-start = (s32[64,64]{1,0:T(8,128)S(1)}, s32[64,64]{1,0:T(8,128)}, u32[]{:S(2)}) copy-start(s32[64,64]{1,0:T(8,128)} %mask.7) | copy-start | bytes 49156
  22.7 5.4 %collective-permute-start.1 = (bf16[2,512,128]{2,1,0:T(8,128)(2,1)S(1)}, bf16[2,512,128]{2,1,0:T(8,128)(2,1)S(1)}, u32[]{:S(2)}, u32[]{:S(2)}) collective-permute-start(bf16[2,512,128]{2,1,0:T(8,128)(2,1)S(1)} %pack_queries.1.qd_a.refs_0_), channel_id=1, source_target_pairs={{0,8},{8,0},{1,9},{9,1},{2,10},{10,2},{3,11},{11,3},{4,12},{12,4},... | collective-permute-start | bytes 786440 | tf_op jit(solution)/shard_map/ppermute | solution.py:268
  24.7 33.4 %collective-permute-start = (bf16[2,512,128]{2,1,0:T(8,128)(2,1)S(1)}, bf16[2,512,128]{2,1,0:T(8,128)(2,1)S(1)}, u32[]{:S(2)}, u32[]{:S(2)}) collective-permute-start(bf16[2,512,128]{2,1,0:T(8,128)(2,1)S(1)} %pack_queries.1.qd_a.refs_0_), channel_id=1, source_target_pairs={{0,64},{64,0},{1,65},{65,1},{2,66},{66,2},{3,67},{67,3},{4,68},{68... | collective-permute-start | bytes 786440 | tf_op jit(solution)/shard_map/ppermute | solution.py:268
  28.1 26.7 %copy-start.3 = (s32[64]{0:T(128)S(1)}, s32[64]{0:T(128)}, u32[]{:S(2)}) copy-start(s32[64]{0:T(128)} %doc.7) | copy-start | bytes 772
  58.1 3.4 %collective-permute-start.2 = (bf16[2,512,128]{2,1,0:T(8,128)(2,1)S(1)}, bf16[2,512,128]{2,1,0:T(8,128)(2,1)S(1)}, u32[]{:S(2)}, u32[]{:S(2)}) collective-permute-start(bf16[2,512,128]{2,1,0:T(8,128)(2,1)S(1)} %collective-permute-done.qd_a.refs_2_), channel_id=1, source_target_pairs={{0,8},{8,0},{1,9},{9,1},{2,10},{10,2},{3,11},{11,3},{4,12},{12,4},... | collective-permute-start | bytes 786440 | tf_op jit(solution)/shard_map/ppermute | solution.py:268
  77.8 41.5 %all-to-all-start.1 = ((bf16[128,16,256]{2,1,0:T(8,128)(2,1)}), bf16[128,16,256]{2,1,0:T(8,128)(2,1)S(1)}, u32[]{:S(2)}, u32[]{:S(2)}) async-start(bf16[128,16,256]{2,1,0:T(8,128)(2,1)} %key_grads.1), calls=%async_computation.1 | async-start | bytes 2097152 | tf_op jit(solution)/shard_map/all_to_all | solution.py:272
  93.0 3.8 %collective-permute-start.3 = (bf16[2,128,1024]{2,1,0:T(8,128)(2,1)S(1)}, bf16[2,128,1024]{2,1,0:T(8,128)(2,1)S(1)}, u32[]{:S(2)}, u32[]{:S(2)}) collective-permute-start(bf16[2,128,1024]{2,1,0:T(8,128)(2,1)S(1)} %get-tuple-element.21), channel_id=1, source_target_pairs={{0,8},{8,0},{1,9},{9,1},{2,10},{10,2},{3,11},{11,3},{4,12},{12,4},... | collective-permute-start | bytes 1572872 | tf_op jit(solution)/shard_map/ppermute | solution.py:268
  97.0 20.5 %collective-permute-start.4 = (bf16[128,1024]{1,0:T(8,128)(2,1)S(1)}, bf16[128,1024]{1,0:T(8,128)(2,1)S(1)}, u32[]{:S(2)}, u32[]{:S(2)}) collective-permute-start(bf16[128,1024]{1,0:T(8,128)(2,1)S(1)} %get-tuple-element.22), channel_id=1, source_target_pairs={{0,64},{64,0},{1,65},{65,1},{2,66},{66,2},{3,67},{67,3},{4,68},{68... | collective-permute-start | bytes 786440 | tf_op jit(solution)/shard_map/ppermute | solution.py:268
